TPU v7x, 512 devices: a whole 4x4x16 slice. The times are simulated.
512 devices in a mesh: dp: 64 (over y_hi, z, core), tensor: 8 (over x, y_lo).
Axes of the slice: x: 4, y: 4 (y_hi: 2, y_lo: 2; y = y_hi * 2 + y_lo), z: 16, core: 2. Of those that a mesh axis runs over, the one named last changes fastest.
Arguments:
- activations: bfloat16 [32768, 7168], P('dp', 'tensor'), may hold values from -6 to 6
- out_grad: bfloat16 [32768, 9216], P('dp', 'tensor'), may hold values from -1 to 1
- projector: float32 [7168, 512], P('tensor'), may hold values from -0.0625 to 0.0625
- moment_one: float32 [512, 9216], P(None, ('tensor', 'dp')), may hold values from -4 to 4
- moment_two: float32 [512, 9216], P(None, ('tensor', 'dp')), may hold values from 0.001 to 0.05
Outputs:
- update: bfloat16 [7168, 9216], P('dp', 'tensor')
- moment_first: float32 [512, 9216], P(None, ('tensor', 'dp'))
- moment_second: float32 [512, 9216], P(None, ('tensor', 'dp'))
All inputs are finite; a program needn't handle non-finite values.
Results may differ from a plain program's by a relative error of at most 0.0057.
Values may be sent and summed in bfloat16 or wider, within the bound.
No kernel may reach another device: no remote copies, remote signals or barrier semaphores. Data moves between devices by JAX's collectives and lax.ppermute only.
A program may use at most 64 MiB of HBM per device.

v0:
```python
import jax
import jax.numpy as jnp
from jax import lax
from jax.sharding import PartitionSpec as P

beta_first = 0.9
beta_second = 0.999
bias_first = 0.999973438601112
bias_second = 0.095207852886291
adam_eps = 1e-08


def broadcast(value, axis, source):
    kept = jnp.where(lax.axis_index(axis) == source, value, 0).astype(value.dtype)
    return lax.psum(kept, axis)


def token_contract(left_side, right_side):
    return lax.dot_general(
        left_side, right_side, (((0,), (0,)), ((), ())), preferred_element_type=jnp.float32
    )


def local(activations, out_grad, projector, moment_one, moment_two):
    partial_proj = jnp.dot(
        activations.astype(jnp.float32), projector, precision=lax.Precision.HIGHEST
    )
    projected = lax.psum(partial_proj, "tensor").astype(jnp.bfloat16)
    partial_grad = token_contract(projected, out_grad)
    gradient = lax.psum_scatter(partial_grad, "dp", scatter_dimension=1, tiled=True)
    moment_first = beta_first * moment_one + (1.0 - beta_first) * gradient
    moment_second = beta_second * moment_two + (1.0 - beta_second) * gradient * gradient
    normed = (
        moment_first / bias_first / (jnp.sqrt(moment_second / bias_second) + adam_eps)
    ).astype(jnp.bfloat16)
    group_size = lax.axis_size("dp") // lax.axis_size("tensor")
    rows_each = projector.shape[0] // group_size
    dp_index = lax.axis_index("dp")
    row_offset = dp_index % group_size * rows_each
    own_slice = lax.dynamic_slice_in_dim(projector, row_offset, rows_each, 0)
    row_basis = broadcast(own_slice, "tensor", dp_index // group_size)
    update = jnp.dot(
        row_basis,
        lax.all_gather(normed, "dp", axis=1, tiled=True).astype(jnp.float32),
        precision=lax.Precision.HIGHEST,
    ).astype(jnp.bfloat16)
    return (update, moment_first, moment_second)


def solution(mesh):
    placed = (
        P("dp", "tensor"),
        P("dp", "tensor"),
        P("tensor", None),
        P(None, ("tensor", "dp")),
        P(None, ("tensor", "dp")),
    )
    return jax.shard_map(
        local,
        mesh=mesh,
        in_specs=placed,
        out_specs=(P("dp", "tensor"), P(None, ("tensor", "dp")), P(None, ("tensor", "dp"))),
        check_vma=False,
    )
```

profile of v0, /device:TPU:1, one launch (start us, length us, event | category | flops | bytes accessed | tf_op | source)
XLA Modules:
  0.0 478.5 jit_solution(12711706191272705806)
XLA Ops:
  8.0 0.0 all-gather.3.cloned.1.call-start
  8.1 3.7 fusion.6
  11.8 57.9 %all-reduce.6 = bf16[512,512]{1,0:T(8,128)(2,1)} all-reduce(f32[512,512]{1,0:T(8,128)S(1)} %fusion.6), channel_id=1, replica_groups=mesh['dp'=64,'tensor'=8] {'tensor'}, use_global_device_ids=true, to_apply=%region_1.0 | all-reduce | flops 262144 | bytes 1572864 | tf_op jit(solution)/shard_map/psum | solution.py:28
  69.7 1.9 fusion.7
  71.6 164.7 %fusion = f32[512,24]{0,1:T(8,128)} fusion(f32[512,1152]{0,1:T(8,128)S(1)} %fusion.7), kind=kCustom, calls=%all-reduce-scatter | all-reduce-scatter fusion | flops 786433 | bytes 2410496
  236.2 0.8 slice
  237.0 1.3 collective-permute-start.15
  238.3 1.9 collective-permute-start
  240.3 1.3 collective-permute-start.1
  241.6 10.7 %collective-permute-start.10 = (f32[512,24]{0,1:T(8,128)}, f32[512,24]{0,1:T(8,128)S(1)}, u32[]{:S(2)}, u32[]{:S(2)}) collective-permute-start(f32[512,24]{0,1:T(8,128)} %fusion), channel_id=1, source_target_pairs={{0,88},{8,96},{16,104},{24,112},{32,120},{40,128},{48,136},{56,144... | collective-permute-start | bytes 147464
  252.3 7.6 %collective-permute-start.11 = (f32[512,24]{0,1:T(8,128)}, f32[512,24]{0,1:T(8,128)S(1)}, u32[]{:S(2)}, u32[]{:S(2)}) collective-permute-start(f32[512,24]{0,1:T(8,128)} %fusion), channel_id=1, source_target_pairs={{0,96},{8,104},{16,112},{24,120},{32,128},{40,136},{48,144},{56,15... | collective-permute-start | bytes 147464
  259.9 1.9 collective-permute-start.12
  261.9 1.6 collective-permute-start.13
  263.5 7.4 %collective-permute-start.14 = (f32[512,24]{0,1:T(8,128)}, f32[512,24]{0,1:T(8,128)S(1)}, u32[]{:S(2)}, u32[]{:S(2)}) collective-permute-start(f32[512,24]{0,1:T(8,128)} %fusion), channel_id=1, source_target_pairs={{0,120},{8,128},{16,136},{24,144},{32,152},{40,160},{48,168},{56,1... | collective-permute-start | bytes 147464
  270.9 5.2 %collective-permute-start.2 = (f32[512,24]{0,1:T(8,128)}, f32[512,24]{0,1:T(8,128)S(1)}, u32[]{:S(2)}, u32[]{:S(2)}) collective-permute-start(f32[512,24]{0,1:T(8,128)} %fusion), channel_id=1, source_target_pairs={{0,24},{8,32},{16,40},{24,48},{32,56},{40,64},{48,72},{56,80},{64,... | collective-permute-start | bytes 147464
  276.2 3.5 collective-permute-start.3
  279.7 7.1 %collective-permute-start.4 = (f32[512,24]{0,1:T(8,128)}, f32[512,24]{0,1:T(8,128)S(1)}, u32[]{:S(2)}, u32[]{:S(2)}) collective-permute-start(f32[512,24]{0,1:T(8,128)} %fusion), channel_id=1, source_target_pairs={{0,40},{8,48},{16,56},{24,64},{32,72},{40,80},{48,88},{56,96},{64,... | collective-permute-start | bytes 147464
  286.8 8.3 %collective-permute-start.5 = (f32[512,24]{0,1:T(8,128)}, f32[512,24]{0,1:T(8,128)S(1)}, u32[]{:S(2)}, u32[]{:S(2)}) collective-permute-start(f32[512,24]{0,1:T(8,128)} %fusion), channel_id=1, source_target_pairs={{0,48},{8,56},{16,64},{24,72},{32,80},{40,88},{48,96},{56,104},{64... | collective-permute-start | bytes 147464
  295.0 5.7 %collective-permute-start.6 = (f32[512,24]{0,1:T(8,128)}, f32[512,24]{0,1:T(8,128)S(1)}, u32[]{:S(2)}, u32[]{:S(2)}) collective-permute-start(f32[512,24]{0,1:T(8,128)} %fusion), channel_id=1, source_target_pairs={{0,56},{8,64},{16,72},{24,80},{32,88},{40,96},{48,104},{56,112},{6... | collective-permute-start | bytes 147464
  300.8 1.9 collective-permute-start.7
  302.8 8.4 %collective-permute-start.8 = (f32[512,24]{0,1:T(8,128)}, f32[512,24]{0,1:T(8,128)S(1)}, u32[]{:S(2)}, u32[]{:S(2)}) collective-permute-start(f32[512,24]{0,1:T(8,128)} %fusion), channel_id=1, source_target_pairs={{0,72},{8,80},{16,88},{24,96},{32,104},{40,112},{48,120},{56,128},... | collective-permute-start | bytes 147464
  311.2 2.8 collective-permute-start.9
  314.1 1.3 dynamic-slice.4
  316.0 0.8 collective-permute-done.9
  316.9 3.0 concatenate
  319.9 0.7 fusion.4
  320.5 0.0 all-reduce.5.cloned.1.call-start
  320.6 1.6 dynamic-slice_select_fusion
  322.3 143.6 %all-gather.3.cloned.1.call-done = bf16[64,18,512]{2,1,0:T(8,128)(2,1)} async-done(((bf16[1,18,512]{2,1,0:T(8,128)(2,1)}), bf16[64,18,512]{2,1,0:T(8,128)(2,1)}) %all-gather.3.cloned.1.call-update) | async-done | bytes 1179664 | tf_op jit(solution)/shard_map/all_gather | solution.py:44
  465.9 2.3 reshape.7
  468.2 0.0 all-reduce.5.cloned.1.call-done
  468.2 2.9 convolution_convert_fusion
  (23 shorter events, 0.1 us)
Async XLA Ops:
  8.0 61.7 %copy-start = (bf16[512,1152]{1,0:T(8,128)(2,1)S(1)}, bf16[512,1152]{1,0:T(8,128)(2,1)}, u32[]{:S(2)}) copy-start(bf16[512,1152]{1,0:T(8,128)(2,1)} %param.6) | copy-start | bytes 3538948
  8.0 457.9 %all-gather.3.cloned.1.call-start = ((), (), s32[]{:S(2)}) async-start(), calls=%async_computation.1 | async-start | bytes 1597440 | tf_op jit(solution)/shard_map/all_gather | solution.py:44
  236.2 83.6 %copy-start.1 = (f32[512,18]{0,1:T(8,128)S(1)}, f32[512,18]{0,1:T(8,128)}, u32[]{:S(2)}) copy-start(f32[512,18]{0,1:T(8,128)} %param.8) | copy-start | bytes 110596
  236.2 83.6 %copy-start.2 = (f32[512,18]{0,1:T(8,128)S(1)}, f32[512,18]{0,1:T(8,128)}, u32[]{:S(2)}) copy-start(f32[512,18]{0,1:T(8,128)} %param.9) | copy-start | bytes 110596
  237.0 22.9 %collective-permute-start.15 = (f32[512,18]{0,1:T(8,128)S(1)}, f32[512,18]{0,1:T(8,128)S(1)}, u32[]{:S(2)}, u32[]{:S(2)}) collective-permute-start(f32[512,18]{0,1:T(8,128)S(1)} %slice), channel_id=1, source_target_pairs={{0,128},{8,136},{16,144},{24,152},{32,160},{40,168},{48,176},{56,1... | collective-permute-start | bytes 110600
  238.3 23.5 %collective-permute-start = (f32[512,24]{0,1:T(8,128)}, f32[512,24]{0,1:T(8,128)S(1)}, u32[]{:S(2)}, u32[]{:S(2)}) collective-permute-start(f32[512,24]{0,1:T(8,128)} %fusion), channel_id=1, source_target_pairs={{0,8},{8,16},{16,24},{24,32},{32,40},{40,48},{48,56},{56,64},{64,7... | collective-permute-start | bytes 147464
  240.3 23.3 %collective-permute-start.1 = (f32[512,24]{0,1:T(8,128)}, f32[512,24]{0,1:T(8,128)S(1)}, u32[]{:S(2)}, u32[]{:S(2)}) collective-permute-start(f32[512,24]{0,1:T(8,128)} %fusion), channel_id=1, source_target_pairs={{0,16},{8,24},{16,32},{24,40},{32,48},{40,56},{48,64},{56,72},{64,... | collective-permute-start | bytes 147464
  241.6 29.4 %collective-permute-start.10 = (f32[512,24]{0,1:T(8,128)}, f32[512,24]{0,1:T(8,128)S(1)}, u32[]{:S(2)}, u32[]{:S(2)}) collective-permute-start(f32[512,24]{0,1:T(8,128)} %fusion), channel_id=1, source_target_pairs={{0,88},{8,96},{16,104},{24,112},{32,120},{40,128},{48,136},{56,144... | collective-permute-start | bytes 147464
  252.3 23.9 %collective-permute-start.11 = (f32[512,24]{0,1:T(8,128)}, f32[512,24]{0,1:T(8,128)S(1)}, u32[]{:S(2)}, u32[]{:S(2)}) collective-permute-start(f32[512,24]{0,1:T(8,128)} %fusion), channel_id=1, source_target_pairs={{0,96},{8,104},{16,112},{24,120},{32,128},{40,136},{48,144},{56,15... | collective-permute-start | bytes 147464
  259.9 19.7 %collective-permute-start.12 = (f32[512,24]{0,1:T(8,128)}, f32[512,24]{0,1:T(8,128)S(1)}, u32[]{:S(2)}, u32[]{:S(2)}) collective-permute-start(f32[512,24]{0,1:T(8,128)} %fusion), channel_id=1, source_target_pairs={{0,104},{8,112},{16,120},{24,128},{32,136},{40,144},{48,152},{56,1... | collective-permute-start | bytes 147464
  261.9 24.9 %collective-permute-start.13 = (f32[512,24]{0,1:T(8,128)}, f32[512,24]{0,1:T(8,128)S(1)}, u32[]{:S(2)}, u32[]{:S(2)}) collective-permute-start(f32[512,24]{0,1:T(8,128)} %fusion), channel_id=1, source_target_pairs={{0,112},{8,120},{16,128},{24,136},{32,144},{40,152},{48,160},{56,1... | collective-permute-start | bytes 147464
  263.5 31.5 %collective-permute-start.14 = (f32[512,24]{0,1:T(8,128)}, f32[512,24]{0,1:T(8,128)S(1)}, u32[]{:S(2)}, u32[]{:S(2)}) collective-permute-start(f32[512,24]{0,1:T(8,128)} %fusion), channel_id=1, source_target_pairs={{0,120},{8,128},{16,136},{24,144},{32,152},{40,160},{48,168},{56,1... | collective-permute-start | bytes 147464
  270.9 29.9 %collective-permute-start.2 = (f32[512,24]{0,1:T(8,128)}, f32[512,24]{0,1:T(8,128)S(1)}, u32[]{:S(2)}, u32[]{:S(2)}) collective-permute-start(f32[512,24]{0,1:T(8,128)} %fusion), channel_id=1, source_target_pairs={{0,24},{8,32},{16,40},{24,48},{32,56},{40,64},{48,72},{56,80},{64,... | collective-permute-start | bytes 147464
  276.2 26.6 %collective-permute-start.3 = (f32[512,24]{0,1:T(8,128)}, f32[512,24]{0,1:T(8,128)S(1)}, u32[]{:S(2)}, u32[]{:S(2)}) collective-permute-start(f32[512,24]{0,1:T(8,128)} %fusion), channel_id=1, source_target_pairs={{0,32},{8,40},{16,48},{24,56},{32,64},{40,72},{48,80},{56,88},{64,... | collective-permute-start | bytes 147464
  279.7 31.6 %collective-permute-start.4 = (f32[512,24]{0,1:T(8,128)}, f32[512,24]{0,1:T(8,128)S(1)}, u32[]{:S(2)}, u32[]{:S(2)}) collective-permute-start(f32[512,24]{0,1:T(8,128)} %fusion), channel_id=1, source_target_pairs={{0,40},{8,48},{16,56},{24,64},{32,72},{40,80},{48,88},{56,96},{64,... | collective-permute-start | bytes 147464
  286.8 29.3 %collective-permute-start.5 = (f32[512,24]{0,1:T(8,128)}, f32[512,24]{0,1:T(8,128)S(1)}, u32[]{:S(2)}, u32[]{:S(2)}) collective-permute-start(f32[512,24]{0,1:T(8,128)} %fusion), channel_id=1, source_target_pairs={{0,48},{8,56},{16,64},{24,72},{32,80},{40,88},{48,96},{56,104},{64... | collective-permute-start | bytes 147464
  295.0 21.0 %collective-permute-start.6 = (f32[512,24]{0,1:T(8,128)}, f32[512,24]{0,1:T(8,128)S(1)}, u32[]{:S(2)}, u32[]{:S(2)}) collective-permute-start(f32[512,24]{0,1:T(8,128)} %fusion), channel_id=1, source_target_pairs={{0,56},{8,64},{16,72},{24,80},{32,88},{40,96},{48,104},{56,112},{6... | collective-permute-start | bytes 147464
  300.8 15.2 %collective-permute-start.7 = (f32[512,24]{0,1:T(8,128)}, f32[512,24]{0,1:T(8,128)S(1)}, u32[]{:S(2)}, u32[]{:S(2)}) collective-permute-start(f32[512,24]{0,1:T(8,128)} %fusion), channel_id=1, source_target_pairs={{0,64},{8,72},{16,80},{24,88},{32,96},{40,104},{48,112},{56,120},{... | collective-permute-start | bytes 147464
  302.8 13.3 %collective-permute-start.8 = (f32[512,24]{0,1:T(8,128)}, f32[512,24]{0,1:T(8,128)S(1)}, u32[]{:S(2)}, u32[]{:S(2)}) collective-permute-start(f32[512,24]{0,1:T(8,128)} %fusion), channel_id=1, source_target_pairs={{0,72},{8,80},{16,88},{24,96},{32,104},{40,112},{48,120},{56,128},... | collective-permute-start | bytes 147464
  311.2 5.6 %collective-permute-start.9 = (f32[512,24]{0,1:T(8,128)}, f32[512,24]{0,1:T(8,128)S(1)}, u32[]{:S(2)}, u32[]{:S(2)}) collective-permute-start(f32[512,24]{0,1:T(8,128)} %fusion), channel_id=1, source_target_pairs={{0,80},{8,88},{16,96},{24,104},{32,112},{40,120},{48,128},{56,136}... | collective-permute-start | bytes 147464
  320.5 147.6 %all-reduce.5.cloned.1.call-start = ((), (), s32[]{:S(2)}) async-start(), calls=%async_computation | async-start | bytes 458752 | tf_op jit(solution)/shard_map/psum | solution.py:15
Sparse Core Ops, SparseCore 0:
  320.7 145.1 all-gather.2
Sparse Core Ops, SparseCore 1:
  324.5 85.7 all-reduce.4
where the time goes:
time: 479 us; the launch traced here: 478 us
  blocking collectives  223 us (47%)
  waiting for transfers between devices  144 us (30%)
  starting transfers between devices  76.9 us (16%)
  between operations  16.5 us (3%)
  matrix products  8.45 us (2%)
  local copies, waits for them, and re-layouts  7.33 us (2%)
    unnamed x1, blocking collectives  165 us
    all_gather x1, waiting for transfers between devices, local(): lax.all_gather(normed, 'dp', axis=1, tiled=True).astype(jnp.float32)  144 us
    unnamed x16, starting transfers between devices  76.8 us
    psum x1, blocking collectives, local(): projected = lax.psum(partial_proj, 'tensor').astype(jnp.bfloat16)  57.9 us
  transfers between devices with their start and end apart: 18, of which 2 were waited for; matrix products, arithmetic and copies ran while one was open for 1% of the time, Pallas kernels for 0%

commit v1 on v0

v1 whole, which is shorter than its diff:
```python
import jax
import jax.numpy as jnp
from jax import lax
from jax.experimental import pallas as pl
from jax.experimental.pallas import tpu as pltpu
from jax.sharding import Mesh, PartitionSpec as P

beta_first = 0.9
beta_second = 0.999
bias_first = 0.999973438601112
bias_second = 0.095207852886291
adam_eps = 1e-08

AXES = ("y_hi", "z_far", "z_near", "core", "x", "y_lo")
SIZES = (2, 8, 2, 2, 4, 2)
DP = AXES[:4]
TENSOR = AXES[4:]
NEAR = ("y_hi", "z_near")
bf16, f32 = jnp.bfloat16, jnp.float32
CORE_SWAP = [(0, 1), (1, 0)]


def swap_cores(value):
    return lax.ppermute(value, "core", CORE_SWAP)


def spread(value, axes, count):
    copies = jnp.broadcast_to(value[None], (count,) + value.shape)
    return lax.all_to_all(copies, axes, 0, 0)


def halves(value, core, axis):
    size = value.shape[axis] // 2
    own = lax.dynamic_slice_in_dim(value, core * size, size, axis)
    other = lax.dynamic_slice_in_dim(value, (1 - core) * size, size, axis)
    return own, other


def in_order(own, other, place, axis):
    return jnp.where(
        place == 0,
        jnp.concatenate([own, other], axis),
        jnp.concatenate([other, own], axis),
    )


def adam(decayed_one, decayed_two, gradient):
    first = decayed_one + (1.0 - beta_first) * gradient
    second = decayed_two + (1.0 - beta_second) * gradient * gradient
    return first, second


def in_two(value):
    high = value.astype(bf16)
    return high, (value - high.astype(f32)).astype(bf16)


def contract(left, right, left_dim, right_dim):
    return lax.dot_general(
        left, right, (((left_dim,), (right_dim,)), ((), ())), preferred_element_type=f32
    )


def project_kernel(start_ref, activations_ref, projector_ref, parts_ref):
    high, low = in_two(projector_ref[...])
    left = activations_ref[...]
    sums = (contract(left, high, 1, 0) + contract(left, low, 1, 0)).astype(bf16)
    few = left.shape[0] // 8
    rows = projector_ref.shape[0] // 8
    start = pl.multiple_of(start_ref[0], 8)
    basis = projector_ref[pl.ds(start, rows), :].astype(bf16)
    for peer in range(8):
        parts_ref[peer, :few, :] = sums[peer * few : (peer + 1) * few]
        if peer < 7:
            parts_ref[peer, few:, :] = basis[peer * 16 : (peer + 1) * 16]
        else:
            parts_ref[peer, few:, :] = jnp.zeros((16, basis.shape[1]), bf16)


def project(activations, projector, row_start):
    tokens, features = activations.shape
    rank = projector.shape[1]
    wide = rank // 2
    few = tokens // 8 + 16
    return pl.pallas_call(
        project_kernel,
        out_shape=jax.ShapeDtypeStruct((8, few, rank), bf16),
        grid_spec=pltpu.PrefetchScalarGridSpec(
            num_scalar_prefetch=1,
            grid=(2,),
            in_specs=[
                pl.BlockSpec((tokens, features), lambda i, _: (0, 0)),
                pl.BlockSpec((features, wide), lambda i, _: (0, i)),
            ],
            out_specs=pl.BlockSpec((8, few, wide), lambda i, _: (0, 0, i)),
        ),
        compiler_params=pltpu.CompilerParams(vmem_limit_bytes=58 << 20),
        name="project",
    )(row_start.reshape(1).astype(jnp.int32), activations, projector)


def gradient_kernel(own_ref, other_ref, both_ref, out_ref, left, total):
    step = pl.program_id(0)
    few = both_ref.shape[2] - 16
    tokens = own_ref.shape[0]
    wide = own_ref.shape[1]

    @pl.when(step == 0)
    def _():
        for side in range(2):
            for peer in range(8):
                left[side, peer * few : (peer + 1) * few, :] = both_ref[peer, side, :few, :]

    sums = contract(own_ref[...], left[0], 0, 0) + contract(other_ref[...], left[1], 0, 0)
    total[pl.ds(pl.multiple_of(step * wide, wide), wide), :] = sums

    @pl.when(step == pl.num_programs(0) - 1)
    def _():
        places, each = out_ref.shape[1], out_ref.shape[2] // 2
        for y_hi in range(2):
            for z_near in range(2):
                for z_far in range(places):
                    at = ((y_hi * places + z_far) * 2 + z_near) * each
                    block = total[at : at + each, :]
                    block = jnp.concatenate([block[:, :128], block[:, 128:]], 0)
                    out_ref[y_hi * 2 + z_near, z_far] = block.astype(bf16)


def gradient_parts(own, other, both):
    tokens, width = own.shape
    half = both.shape[3]
    steps = 3
    wide = width // steps
    out = (4, 8, width // 16, half // 2)
    return pl.pallas_call(
        gradient_kernel,
        out_shape=jax.ShapeDtypeStruct(out, bf16),
        grid=(steps,),
        in_specs=[
            pl.BlockSpec((tokens, wide), lambda i: (0, i)),
            pl.BlockSpec((tokens, wide), lambda i: (0, i)),
            pl.BlockSpec(both.shape, lambda i: (0, 0, 0, 0)),
        ],
        out_specs=pl.BlockSpec(out, lambda i: (0, 0, 0, 0)),
        scratch_shapes=[
            pltpu.VMEM((2, tokens, half), bf16),
            pltpu.VMEM((width, half), f32),
        ],
        compiler_params=pltpu.CompilerParams(vmem_limit_bytes=40 << 20),
        name="gradient",
    )(own, other, both)


def step_kernel(far_ref, moments_ref, normed_ref, total_ref):
    total = jnp.sum(far_ref[...].astype(f32), axis=0)
    each = total.shape[0] // 2
    for part in range(2):
        total_ref[part] = total[part * each : (part + 1) * each]
    decayed = [jnp.concatenate([moments_ref[i, 0], moments_ref[i, 1]], 0) for i in range(2)]
    first, second = adam(decayed[0], decayed[1], total)
    normed = first / bias_first / (jnp.sqrt(second / bias_second) + adam_eps)
    normed = normed.astype(bf16)
    for place in range(8):
        normed_ref[place] = normed


def step(far, moments):
    return pl.pallas_call(
        step_kernel,
        out_shape=(
            jax.ShapeDtypeStruct(far.shape, bf16),
            jax.ShapeDtypeStruct(moments.shape[1:], f32),
        ),
        name="step",
    )(far, moments)


def local(activations, out_grad, projector, moment_one, moment_two):
    y_hi = lax.axis_index("y_hi")
    z_far = lax.axis_index("z_far")
    z_near = lax.axis_index("z_near")
    core = lax.axis_index("core")
    tokens, rank, width = out_grad.shape[0], projector.shape[1], out_grad.shape[1]
    half = rank // 2
    each = width // 32
    few = tokens // 8
    rows = projector.shape[0] // 8

    row_start = ((z_far % 2) * 4 + z_near * 2 + core) * rows
    parts = project(activations, projector, row_start)
    parts, out_grad, moment_one, moment_two = lax.optimization_barrier(
        (parts, out_grad, moment_one, moment_two)
    )
    parts = lax.all_to_all(parts, TENSOR, 0, 0)

    grad_other = swap_cores(out_grad)
    moments = jnp.stack([beta_first * moment_one.T, beta_second * moment_two.T])
    keep, send = halves(moments.reshape(2, each // 2, 4, 128).transpose(0, 2, 1, 3), core, 1)
    moments = in_order(keep, swap_cores(send), core, 2)
    summed = parts[:, :few].astype(f32).sum(0).astype(bf16)
    row_part = lax.dynamic_index_in_dim(parts[:, few:], y_hi * 4 + z_far // 2, 0, keepdims=False)
    summed, moments = lax.optimization_barrier((summed, moments))

    own, other = halves(summed, core, 1)
    both = jnp.stack([own, swap_cores(other)])
    both = jnp.concatenate([both, jnp.stack(halves(row_part, core, 1))], 1)
    both = spread(both, TENSOR, 8)
    row_basis = both[:7, :, few:]

    near = lax.all_to_all(gradient_parts(out_grad, grad_other, both), NEAR, 0, 0)
    near = near.astype(f32).sum(0).astype(bf16)
    far = lax.all_to_all(near, "z_far", 0, 0)
    normed, total = step(far, moments)
    normed = lax.all_to_all(normed, "z_far", 0, 0)

    back_own, back_other = halves(total, core, 1)
    own_gradient = in_order(back_own, swap_cores(back_other), core, 0)
    normed, own_gradient = lax.optimization_barrier((normed, own_gradient))
    own_gradient = own_gradient.transpose(1, 0, 2).reshape(each // 2, rank).T
    moment_first, moment_second = adam(
        beta_first * moment_one, beta_second * moment_two, own_gradient
    )

    normed_own = spread(normed, NEAR, 4).reshape(2, 2, 8, 2, each, 128)
    normed_own = normed_own.transpose(0, 2, 1, 4, 3, 5).reshape(width, half)
    normed_other = swap_cores(normed_own)
    update = 0.0
    for side, half_step in enumerate((normed_own, normed_other)):
        update = update + contract(row_basis[:, side].reshape(rows, half), half_step, 1, 1)
    return (update.astype(bf16), moment_first, moment_second)


def solution(mesh):
    fine = Mesh(mesh.devices.reshape(SIZES), AXES)
    placed = (
        P(DP, TENSOR),
        P(DP, TENSOR),
        P(TENSOR, None),
        P(None, TENSOR + DP),
        P(None, TENSOR + DP),
    )
    return jax.shard_map(
        local,
        mesh=fine,
        in_specs=placed,
        out_specs=(P(DP, TENSOR), P(None, TENSOR + DP), P(None, TENSOR + DP)),
        check_vma=False,
    )
```

time: 479 us -> 123 us (0.26)
  blocking collectives: 223 us -> 63.3 us
  waiting for transfers between devices: 144 us -> 7.02 us
  starting transfers between devices: 76.9 us -> 39.1 us
  between operations: 16.5 us -> 0.92 us
  matrix products: 8.45 us -> 1.34 us
  Pallas kernels: 0 us -> 6.98 us
  local copies, waits for them, and re-layouts: 7.33 us -> 1.78 us
    unnamed x1 -> x0, blocking collectives: 165 us -> none
    all_gather x1 -> x0, waiting for transfers between devices: 144 us -> none  [local(): lax.all_gather(normed, 'dp', axis=1, tiled=True).astype(jnp.float32)]
    unnamed x16 -> x0, starting transfers between devices: 76.8 us -> none
    all_to_all x0 -> x4, blocking collectives: none -> 63.3 us  [the longest x1 27.5 us: local(): far = lax.all_to_all(near, 'z_far', 0, 0)]
    psum x1 -> x0, blocking collectives: 57.9 us -> none  [local(): projected = lax.psum(partial_proj, 'tensor').astype(jnp.bfloat16)]
    ppermute x0 -> x5, starting transfers between devices: none -> 29.7 us  [swap_cores(): return lax.ppermute(value, 'core', CORE_SWAP)]
    all_to_all x0 -> x2, starting transfers between devices: none -> 9.38 us  [the longest x1 6 us: local(): parts = lax.all_to_all(parts, TENSOR, 0, 0)]
    unnamed x10, local copies, waits for them, and re-layouts: 7.33 us -> 0.12 us
  transfers between devices with their start and end apart: 18 -> 7, of which waited for: 2 -> 4; matrix products, arithmetic and copies ran while one was open for 1% -> 2% of each run, Pallas kernels for 0% -> 0%
where the time goes in v1:
time: 123 us; the launch traced here: 122 us
  blocking collectives  63.3 us (51%)
  starting transfers between devices  39.1 us (32%)
  waiting for transfers between devices  7.02 us (6%)
  Pallas kernels  6.98 us (6%)
  local copies, waits for them, and re-layouts  1.78 us (1%)
  other arithmetic  1.49 us (1%)
  matrix products  1.34 us (1%)
    ppermute x5, starting transfers between devices, swap_cores(): return lax.ppermute(value, 'core', CORE_SWAP)  29.7 us
    all_to_all x1, blocking collectives, local(): far = lax.all_to_all(near, 'z_far', 0, 0)  27.5 us
    all_to_all x2, blocking collectives, spread(): return lax.all_to_all(copies, axes, 0, 0)  23.5 us
    all_to_all x1, blocking collectives, local(): lax.all_to_all(gradient_parts(out_grad, grad_other, both), NEAR, 0, 0)  12.2 us
    all_to_all x1, starting transfers between devices, local(): parts = lax.all_to_all(parts, TENSOR, 0, 0)  6 us
    all_to_all x1, waiting for transfers between devices, local(): normed = lax.all_to_all(normed, 'z_far', 0, 0)  4.89 us
    pallas_call x1, Pallas kernels, project(): pl.pallas_call(project_kernel, out_shape=jax.ShapeDtypeStruct((8, few, ra...  3.65 us
    all_to_all x1, starting transfers between devices, local(): normed = lax.all_to_all(normed, 'z_far', 0, 0)  3.38 us
  transfers between devices with their start and end apart: 7, of which 4 were waited for; matrix products, arithmetic and copies ran while one was open for 2% of the time, Pallas kernels for 0%

profile of v1, /device:TPU:1, one launch (start us, length us, event | category | flops | bytes accessed | tf_op | source)
XLA Modules:
  0.0 121.9 jit_solution(16722487944334797427)
XLA Ops:
  0.6 3.6 %project.1 = bf16[8,80,512]{2,1,0:T(8,128)(2,1)} custom-call(s32[1]{0:T(128)} %bitcast.start_ref, bf16[512,896]{1,0:T(8,128)(2,1)} %activations_ref.1, f32[896,512]{1,0:T(8,128)} %projector_ref.1), custom_call_target="tpu_custom_call" | custom-call | tf_op jit(solution)/shard_map/project/pallas_call | solution.py:85
  4.3 6.0 %all-to-all-start = ((bf16[8,80,512]{2,1,0:T(8,128)(2,1)}), bf16[8,80,512]{2,1,0:T(8,128)(2,1)S(1)}, u32[]{:S(2)}, u32[]{:S(2)}) async-start(bf16[8,80,512]{2,1,0:T(8,128)(2,1)} %project.1), calls=%async_computation | async-start | bytes 1310720 | tf_op jit(solution)/shard_map/all_to_all | solution.py:194
  10.5 6.5 %collective-permute-start = (f32[2,2,18,128]{3,2,1,0:T(8,128)S(1)}, f32[2,2,18,128]{3,2,1,0:T(8,128)S(1)}, u32[]{:S(2)}, u32[]{:S(2)}) collective-permute-start(f32[2,2,18,128]{3,2,1,0:T(8,128)S(1)} %get-tuple-element.28), channel_id=1, source_target_pairs={{0,8},{8,0},{1,9},{9,1},{2,10},{10,2},{3,11},{11,3},{4,12},{12,4},... | collective-permute-start | bytes 110600 | tf_op jit(solution)/shard_map/ppermute | solution.py:24
  16.9 1.9 %collective-permute-start.2 = (bf16[512,1152]{1,0:T(8,128)(2,1)S(1)}, bf16[512,1152]{1,0:T(8,128)(2,1)S(1)}, u32[]{:S(2)}, u32[]{:S(2)}) collective-permute-start(bf16[512,1152]{1,0:T(8,128)(2,1)S(1)} %copy-done), channel_id=1, source_target_pairs={{0,8},{8,0},{1,9},{9,1},{2,10},{10,2},{3,11},{11,3},{4,12},{12,4},... | collective-permute-start | bytes 3538952 | tf_op jit(solution)/shard_map/ppermute | solution.py:24
  18.9 0.0 collective-permute-done
  18.9 0.6 maximum_select_fusion.moments_ref
  19.6 0.0 all-to-all-done
  19.6 0.1 slice_reduce_fusion
  19.7 6.0 %collective-permute-start.1 = (bf16[64,256]{1,0:T(8,128)(2,1)S(1)}, bf16[64,256]{1,0:T(8,128)(2,1)S(1)}, u32[]{:S(2)}, u32[]{:S(2)}) collective-permute-start(bf16[64,256]{1,0:T(8,128)(2,1)S(1)} %get-tuple-element.30), channel_id=1, source_target_pairs={{0,8},{8,0},{1,9},{9,1},{2,10},{10,2},{3,11},{11,3},{4,12},{12,4},... | collective-permute-start | bytes 98312 | tf_op jit(solution)/shard_map/ppermute | solution.py:24
  25.7 0.1 constant_dynamic-slice_fusion.3
  25.8 0.7 collective-permute-done.1
  26.6 13.1 %all_to_all.30.both_ref = bf16[8,2,80,256]{3,2,1,0:T(8,128)(2,1)S(1)} all-to-all(bf16[8,2,80,256]{3,2,1,0:T(8,128)(2,1)S(1)} %broadcast_in_dim.4), channel_id=1, replica_groups=mesh['y_hi'=2,'z_far'=8,'z_near'=2,'core'=2,'x'=4,'y_lo'=2] {'x','y_lo'}, dimensions={0} | all-to-all | bytes 1310720 | tf_op jit(solution)/shard_map/all_to_all | solution.py:29
  39.8 0.0 collective-permute-done.2.other_ref
  39.8 1.7 %gradient.1 = bf16[4,8,72,128]{3,2,1,0:T(8,128)(2,1)S(1)} custom-call(bf16[512,1152]{1,0:T(8,128)(2,1)S(1)} %copy-done, bf16[512,1152]{1,0:T(8,128)(2,1)S(1)} %collective-permute-done.2.other_ref, bf16[8,2,80,256]{3,2,1,0:T(8,128)(2,1)S(1)} %all_to_all.30.both_ref), custom_call_target="tpu_custom_call" | custom-call | tf_op jit(solution)/shard_map/gradient/pallas_call | solution.py:135
  41.4 12.2 %all_to_all.31 = bf16[4,8,72,128]{3,2,1,0:T(8,128)(2,1)S(1)} all-to-all(bf16[4,8,72,128]{3,2,1,0:T(8,128)(2,1)S(1)} %gradient.1), channel_id=1, replica_groups=mesh['y_hi'=2,'z_far'=8,'z_near'=2,'core'=2,'x'=4,'y_lo'=2] {'y_hi','z_n..., dimensions={0} | all-to-all | bytes 1179648 | tf_op jit(solution)/shard_map/all_to_all | solution.py:210
  53.7 0.1 reduce_sum.25
  53.8 27.5 %all_to_all.32.far_ref = bf16[8,72,128]{2,1,0:T(8,128)(2,1)} all-to-all(bf16[8,72,128]{2,1,0:T(8,128)(2,1)S(1)} %reduce_sum.25), channel_id=1, replica_groups=mesh['y_hi'=2,'z_far'=8,'z_near'=2,'core'=2,'x'=4,'y_lo'=2] {'z_far'}, dimensions={0} | all-to-all | bytes 294912 | tf_op jit(solution)/shard_map/all_to_all | solution.py:212
  81.3 1.7 %step.1 = (bf16[8,72,128]{2,1,0:T(8,128)(2,1)}, f32[2,36,128]{2,1,0:T(8,128)}) custom-call(bf16[8,72,128]{2,1,0:T(8,128)(2,1)} %all_to_all.32.far_ref, f32[2,2,36,128]{3,2,1,0:T(8,128)} %maximum_select_fusion.moments_ref), custom_call_target="tpu_custom_call" | custom-call | tf_op jit(solution)/shard_map/step/pallas_call | solution.py:168
  83.0 3.4 %all-to-all-start.4 = ((bf16[8,72,128]{2,1,0:T(8,128)(2,1)}), bf16[8,72,128]{2,1,0:T(8,128)(2,1)S(1)}, u32[]{:S(2)}, u32[]{:S(2)}) async-start(bf16[8,72,128]{2,1,0:T(8,128)(2,1)} %get-tuple-element.19), calls=%async_computation.4 | async-start | bytes 294912 | tf_op jit(solution)/shard_map/all_to_all | solution.py:214
  86.4 0.9 constant_dynamic-slice_fusion.1
  87.2 6.4 %collective-permute-start.3 = (f32[2,18,128]{2,1,0:T(8,128)S(1)}, f32[2,18,128]{2,1,0:T(8,128)S(1)}, u32[]{:S(2)}, u32[]{:S(2)}) collective-permute-start(f32[2,18,128]{2,1,0:T(8,128)S(1)} %get-tuple-element.34), channel_id=1, source_target_pairs={{0,8},{8,0},{1,9},{9,1},{2,10},{10,2},{3,11},{11,3},{4,12},{12,4},... | collective-permute-start | bytes 55304 | tf_op jit(solution)/shard_map/ppermute | solution.py:24
  93.6 0.8 collective-permute-done.3
  94.5 4.9 %all-to-all-done.4 = bf16[8,72,128]{2,1,0:T(8,128)(2,1)S(1)} async-done(((bf16[8,72,128]{2,1,0:T(8,128)(2,1)}), bf16[8,72,128]{2,1,0:T(8,128)(2,1)S(1)}, u32[]{:S(2)}, u32[]{:S(2)}) %all-to-all-start.4) | async-done | bytes 147488 | tf_op jit(solution)/shard_map/all_to_all | solution.py:214
  99.4 0.1 broadcast_in_dim.5
  99.5 10.4 %all_to_all.33 = bf16[4,8,72,128]{3,1,2,0:T(8,128)(2,1)S(1)} all-to-all(bf16[4,8,72,128]{3,1,2,0:T(8,128)(2,1)S(1)} %broadcast_in_dim.5), channel_id=1, replica_groups=mesh['y_hi'=2,'z_far'=8,'z_near'=2,'core'=2,'x'=4,'y_lo'=2] {'y_hi','z_n..., dimensions={0} | all-to-all | bytes 1179648 | tf_op jit(solution)/shard_map/all_to_all | solution.py:29
  109.9 0.5 copy.11
  110.3 0.1 copy.19
  110.4 8.9 %collective-permute-start.4 = (bf16[1152,256]{1,0:T(8,128)(2,1)S(1)}, bf16[1152,256]{1,0:T(8,128)(2,1)S(1)}, u32[]{:S(2)}, u32[]{:S(2)}) collective-permute-start(bf16[1152,256]{1,0:T(8,128)(2,1)S(1)} %bitcast.38), channel_id=1, source_target_pairs={{0,8},{8,0},{1,9},{9,1},{2,10},{10,2},{3,11},{11,3},{4,12},{12,4},... | collective-permute-start | bytes 1769480 | tf_op jit(solution)/shard_map/ppermute | solution.py:24
  119.4 0.7 fusion.1
  120.0 0.3 fusion.3
  120.3 0.6 collective-permute-done.4
  120.9 1.0 fusion
  (22 shorter events, 0.2 us)
Async XLA Ops:
  4.3 6.0 %copy-start.1 = (f32[512,18]{0,1:T(8,128)S(1)}, f32[512,18]{0,1:T(8,128)}, u32[]{:S(2)}) copy-start(f32[512,18]{0,1:T(8,128)} %param.9) | copy-start | bytes 110596
  4.3 6.0 %copy-start.2 = (f32[512,18]{0,1:T(8,128)S(1)}, f32[512,18]{0,1:T(8,128)}, u32[]{:S(2)}) copy-start(f32[512,18]{0,1:T(8,128)} %param.8) | copy-start | bytes 110596
  4.3 12.6 %copy-start = (bf16[512,1152]{1,0:T(8,128)(2,1)S(1)}, bf16[512,1152]{1,0:T(8,128)(2,1)}, u32[]{:S(2)}) copy-start(bf16[512,1152]{1,0:T(8,128)(2,1)} %own_ref) | copy-start | bytes 3538948
  4.3 15.3 %all-to-all-start = ((bf16[8,80,512]{2,1,0:T(8,128)(2,1)}), bf16[8,80,512]{2,1,0:T(8,128)(2,1)S(1)}, u32[]{:S(2)}, u32[]{:S(2)}) async-start(bf16[8,80,512]{2,1,0:T(8,128)(2,1)} %project.1), calls=%async_computation | async-start | bytes 1310720 | tf_op jit(solution)/shard_map/all_to_all | solution.py:194
  10.5 8.5 %collective-permute-start = (f32[2,2,18,128]{3,2,1,0:T(8,128)S(1)}, f32[2,2,18,128]{3,2,1,0:T(8,128)S(1)}, u32[]{:S(2)}, u32[]{:S(2)}) collective-permute-start(f32[2,2,18,128]{3,2,1,0:T(8,128)S(1)} %get-tuple-element.28), channel_id=1, source_target_pairs={{0,8},{8,0},{1,9},{9,1},{2,10},{10,2},{3,11},{11,3},{4,12},{12,4},... | collective-permute-start | bytes 110600 | tf_op jit(solution)/shard_map/ppermute | solution.py:24
  16.9 22.8 %collective-permute-start.2 = (bf16[512,1152]{1,0:T(8,128)(2,1)S(1)}, bf16[512,1152]{1,0:T(8,128)(2,1)S(1)}, u32[]{:S(2)}, u32[]{:S(2)}) collective-permute-start(bf16[512,1152]{1,0:T(8,128)(2,1)S(1)} %copy-done), channel_id=1, source_target_pairs={{0,8},{8,0},{1,9},{9,1},{2,10},{10,2},{3,11},{11,3},{4,12},{12,4},... | collective-permute-start | bytes 3538952 | tf_op jit(solution)/shard_map/ppermute | solution.py:24
  19.7 6.9 %collective-permute-start.1 = (bf16[64,256]{1,0:T(8,128)(2,1)S(1)}, bf16[64,256]{1,0:T(8,128)(2,1)S(1)}, u32[]{:S(2)}, u32[]{:S(2)}) collective-permute-start(bf16[64,256]{1,0:T(8,128)(2,1)S(1)} %get-tuple-element.30), channel_id=1, source_target_pairs={{0,8},{8,0},{1,9},{9,1},{2,10},{10,2},{3,11},{11,3},{4,12},{12,4},... | collective-permute-start | bytes 98312 | tf_op jit(solution)/shard_map/ppermute | solution.py:24
  83.0 16.4 %all-to-all-start.4 = ((bf16[8,72,128]{2,1,0:T(8,128)(2,1)}), bf16[8,72,128]{2,1,0:T(8,128)(2,1)S(1)}, u32[]{:S(2)}, u32[]{:S(2)}) async-start(bf16[8,72,128]{2,1,0:T(8,128)(2,1)} %get-tuple-element.19), calls=%async_computation.4 | async-start | bytes 294912 | tf_op jit(solution)/shard_map/all_to_all | solution.py:214
  87.2 7.2 %collective-permute-start.3 = (f32[2,18,128]{2,1,0:T(8,128)S(1)}, f32[2,18,128]{2,1,0:T(8,128)S(1)}, u32[]{:S(2)}, u32[]{:S(2)}) collective-permute-start(f32[2,18,128]{2,1,0:T(8,128)S(1)} %get-tuple-element.34), channel_id=1, source_target_pairs={{0,8},{8,0},{1,9},{9,1},{2,10},{10,2},{3,11},{11,3},{4,12},{12,4},... | collective-permute-start | bytes 55304 | tf_op jit(solution)/shard_map/ppermute | solution.py:24
  110.4 10.5 %collective-permute-start.4 = (bf16[1152,256]{1,0:T(8,128)(2,1)S(1)}, bf16[1152,256]{1,0:T(8,128)(2,1)S(1)}, u32[]{:S(2)}, u32[]{:S(2)}) collective-permute-start(bf16[1152,256]{1,0:T(8,128)(2,1)S(1)} %bitcast.38), channel_id=1, source_target_pairs={{0,8},{8,0},{1,9},{9,1},{2,10},{10,2},{3,11},{11,3},{4,12},{12,4},... | collective-permute-start | bytes 1769480 | tf_op jit(solution)/shard_map/ppermute | solution.py:24

commit v2 on v1

--- a/solution.py
+++ b/solution.py
@@ -11,13 +11,22 @@
 bias_second = 0.095207852886291
 adam_eps = 1e-08
 
-AXES = ("y_hi", "z_far", "z_near", "core", "x", "y_lo")
-SIZES = (2, 8, 2, 2, 4, 2)
-DP = AXES[:4]
-TENSOR = AXES[4:]
-NEAR = ("y_hi", "z_near")
+AXES = ("y_hi", "z3", "z2", "z1", "z0", "core", "x", "y_lo")
+SIZES = (2, 2, 2, 2, 2, 2, 4, 2)
+DP = AXES[:6]
+TENSOR = AXES[6:]
+SUMMING = ("x", "y_lo")
+NEAR = ("y_hi", "z0")
+FAR = ("z1", "z2", "z3")
 bf16, f32 = jnp.bfloat16, jnp.float32
 CORE_SWAP = [(0, 1), (1, 0)]
+
+
+def place_in(axes, coords):
+    index = 0
+    for axis in axes:
+        index = index * SIZES[AXES.index(axis)] + coords[axis]
+    return index
 
 
 def swap_cores(value):
@@ -101,7 +110,8 @@
 
 def gradient_kernel(own_ref, other_ref, both_ref, out_ref, left, total):
     step = pl.program_id(0)
-    few = both_ref.shape[2] - 16
+    few = both_ref.shape[1] - 16
+    half = left.shape[2]
     tokens = own_ref.shape[0]
     wide = own_ref.shape[1]
 
@@ -109,26 +119,26 @@
     def _():
         for side in range(2):
             for peer in range(8):
-                left[side, peer * few : (peer + 1) * few, :] = both_ref[peer, side, :few, :]
+                left[side, peer * few : (peer + 1) * few, :] = both_ref[
+                    peer, :few, side * half : (side + 1) * half
+                ]
 
     sums = contract(own_ref[...], left[0], 0, 0) + contract(other_ref[...], left[1], 0, 0)
     total[pl.ds(pl.multiple_of(step * wide, wide), wide), :] = sums
 
     @pl.when(step == pl.num_programs(0) - 1)
     def _():
-        places, each = out_ref.shape[1], out_ref.shape[2] // 2
-        for y_hi in range(2):
-            for z_near in range(2):
-                for z_far in range(places):
-                    at = ((y_hi * places + z_far) * 2 + z_near) * each
-                    block = total[at : at + each, :]
-                    block = jnp.concatenate([block[:, :128], block[:, 128:]], 0)
-                    out_ref[y_hi * 2 + z_near, z_far] = block.astype(bf16)
+        each = out_ref.shape[2] // 2
+        for index in range(total.shape[0] // each):
+            coords = {axis: index >> (4 - bit) & 1 for bit, axis in enumerate(AXES[:5])}
+            block = total[index * each : (index + 1) * each, :]
+            block = jnp.concatenate([block[:, :128], block[:, 128:]], 0)
+            out_ref[place_in(NEAR, coords), place_in(FAR, coords)] = block.astype(bf16)
 
 
 def gradient_parts(own, other, both):
     tokens, width = own.shape
-    half = both.shape[3]
+    half = both.shape[2] // 2
     steps = 3
     wide = width // steps
     out = (4, 8, width // 16, half // 2)
@@ -139,7 +149,7 @@
         in_specs=[
             pl.BlockSpec((tokens, wide), lambda i: (0, i)),
             pl.BlockSpec((tokens, wide), lambda i: (0, i)),
-            pl.BlockSpec(both.shape, lambda i: (0, 0, 0, 0)),
+            pl.BlockSpec(both.shape, lambda i: (0, 0, 0)),
         ],
         out_specs=pl.BlockSpec(out, lambda i: (0, 0, 0, 0)),
         scratch_shapes=[
@@ -176,42 +186,40 @@
 
 
 def local(activations, out_grad, projector, moment_one, moment_two):
-    y_hi = lax.axis_index("y_hi")
-    z_far = lax.axis_index("z_far")
-    z_near = lax.axis_index("z_near")
-    core = lax.axis_index("core")
+    y_hi, z3, z2, z1, z0, core = (lax.axis_index(axis) for axis in DP)
     tokens, rank, width = out_grad.shape[0], projector.shape[1], out_grad.shape[1]
     half = rank // 2
     each = width // 32
     few = tokens // 8
     rows = projector.shape[0] // 8
 
-    row_start = ((z_far % 2) * 4 + z_near * 2 + core) * rows
+    row_start = (z1 * 4 + z0 * 2 + core) * rows
     parts = project(activations, projector, row_start)
     parts, out_grad, moment_one, moment_two = lax.optimization_barrier(
         (parts, out_grad, moment_one, moment_two)
     )
-    parts = lax.all_to_all(parts, TENSOR, 0, 0)
+    parts = lax.all_to_all(parts, SUMMING, 0, 0)
 
     grad_other = swap_cores(out_grad)
     moments = jnp.stack([beta_first * moment_one.T, beta_second * moment_two.T])
     keep, send = halves(moments.reshape(2, each // 2, 4, 128).transpose(0, 2, 1, 3), core, 1)
     moments = in_order(keep, swap_cores(send), core, 2)
     summed = parts[:, :few].astype(f32).sum(0).astype(bf16)
-    row_part = lax.dynamic_index_in_dim(parts[:, few:], y_hi * 4 + z_far // 2, 0, keepdims=False)
+    holder = place_in(SUMMING, {"x": y_hi * 2 + z3, "y_lo": z2})
+    row_part = lax.dynamic_index_in_dim(parts[:, few:], holder, 0, keepdims=False)
     summed, moments = lax.optimization_barrier((summed, moments))
 
     own, other = halves(summed, core, 1)
-    both = jnp.stack([own, swap_cores(other)])
-    both = jnp.concatenate([both, jnp.stack(halves(row_part, core, 1))], 1)
-    both = spread(both, TENSOR, 8)
-    row_basis = both[:7, :, few:]
-
-    near = lax.all_to_all(gradient_parts(out_grad, grad_other, both), NEAR, 0, 0)
-    near = near.astype(f32).sum(0).astype(bf16)
-    far = lax.all_to_all(near, "z_far", 0, 0)
+    both = jnp.concatenate([own, swap_cores(other)], 1)
+    both = jnp.concatenate([both, jnp.concatenate(halves(row_part, core, 1), 1)], 0)
+    both = spread(both, SUMMING, 8)
+    row_basis = both[:7, few:].reshape(rows, rank)
+
+    near = gradient_parts(out_grad, grad_other, both).reshape(4, 16 * each, 128)
+    near = lax.all_to_all(near, NEAR, 0, 0).astype(f32).sum(0).astype(bf16)
+    far = lax.all_to_all(near.reshape(8, 2 * each, 128), FAR, 0, 0)
     normed, total = step(far, moments)
-    normed = lax.all_to_all(normed, "z_far", 0, 0)
+    normed = lax.all_to_all(normed, FAR, 0, 0)
 
     back_own, back_other = halves(total, core, 1)
     own_gradient = in_order(back_own, swap_cores(back_other), core, 0)
@@ -221,12 +229,15 @@
         beta_first * moment_one, beta_second * moment_two, own_gradient
     )
 
-    normed_own = spread(normed, NEAR, 4).reshape(2, 2, 8, 2, each, 128)
-    normed_own = normed_own.transpose(0, 2, 1, 4, 3, 5).reshape(width, half)
+    normed = spread(normed.reshape(16 * each, 128), NEAR, 4)
+    normed = normed.reshape((2,) * 6 + (each, 128))
+    order = [(NEAR + FAR).index(axis) for axis in AXES[:5]]
+    normed_own = normed.transpose(*order, 6, 5, 7).reshape(width, half)
     normed_other = swap_cores(normed_own)
     update = 0.0
     for side, half_step in enumerate((normed_own, normed_other)):
-        update = update + contract(row_basis[:, side].reshape(rows, half), half_step, 1, 1)
+        left = row_basis[:, side * half : (side + 1) * half]
+        update = update + contract(left, half_step, 1, 1)
     return (update.astype(bf16), moment_first, moment_second)
 
 

time: 123 us -> 121 us (0.984)
  blocking collectives: 63.3 us -> 61.4 us
    all_to_all x2, blocking collectives: 39.8 us -> 37.9 us  [the longest x1 25.6 us: local(): far = lax.all_to_all(near.reshape(8, 2 * each, 128), FAR, 0, 0)]
where the time goes in v2:
time: 121 us; the launch traced here: 120 us
  blocking collectives  61.4 us (51%)
  starting transfers between devices  40 us (33%)
  Pallas kernels  6.99 us (6%)
  waiting for transfers between devices  6.12 us (5%)
  local copies, waits for them, and re-layouts  2.21 us (2%)
  other arithmetic  1.5 us (1%)
  matrix products  1.34 us (1%)
    ppermute x5, starting transfers between devices, swap_cores(): return lax.ppermute(value, 'core', CORE_SWAP)  29.4 us
    all_to_all x1, blocking collectives, local(): far = lax.all_to_all(near.reshape(8, 2 * each, 128), FAR, 0, 0)  25.6 us
    all_to_all x2, blocking collectives, spread(): return lax.all_to_all(copies, axes, 0, 0)  23.5 us
    all_to_all x1, blocking collectives, local(): near = lax.all_to_all(near, NEAR, 0, 0).astype(f32).sum(0).astype(bf16)  12.3 us
    all_to_all x1, starting transfers between devices, local(): parts = lax.all_to_all(parts, SUMMING, 0, 0)  6 us
    all_to_all x1, starting transfers between devices, local(): normed = lax.all_to_all(normed, FAR, 0, 0)  4.54 us
    all_to_all x1, waiting for transfers between devices, local(): normed = lax.all_to_all(normed, FAR, 0, 0)  3.99 us
    pallas_call x1, Pallas kernels, project(): pl.pallas_call(project_kernel, out_shape=jax.ShapeDtypeStruct((8, few, ra...  3.65 us
  transfers between devices with their start and end apart: 7, of which 4 were waited for; matrix products, arithmetic and copies ran while one was open for 2% of the time, Pallas kernels for 0%

profile of v2, /device:TPU:1, one launch (start us, length us, event | category | flops | bytes accessed | tf_op | source)
XLA Modules:
  0.0 120.4 jit_solution(9120431752632413969)
XLA Ops:
  0.6 3.7 %project.1 = bf16[8,80,512]{2,1,0:T(8,128)(2,1)} custom-call(s32[1]{0:T(128)} %bitcast.start_ref, bf16[512,896]{1,0:T(8,128)(2,1)} %activations_ref.1, f32[896,512]{1,0:T(8,128)} %projector_ref.1), custom_call_target="tpu_custom_call" | custom-call | tf_op jit(solution)/shard_map/project/pallas_call | solution.py:94
  4.3 6.0 %all-to-all-start = ((bf16[8,80,512]{2,1,0:T(8,128)(2,1)}), bf16[8,80,512]{2,1,0:T(8,128)(2,1)S(1)}, u32[]{:S(2)}, u32[]{:S(2)}) async-start(bf16[8,80,512]{2,1,0:T(8,128)(2,1)} %project.1), calls=%async_computation | async-start | bytes 1310720 | tf_op jit(solution)/shard_map/all_to_all | solution.py:201
  10.4 6.5 %collective-permute-start = (f32[2,2,18,128]{3,2,1,0:T(8,128)S(1)}, f32[2,2,18,128]{3,2,1,0:T(8,128)S(1)}, u32[]{:S(2)}, u32[]{:S(2)}) collective-permute-start(f32[2,2,18,128]{3,2,1,0:T(8,128)S(1)} %get-tuple-element.26), channel_id=1, source_target_pairs={{0,8},{8,0},{1,9},{9,1},{2,10},{10,2},{3,11},{11,3},{4,12},{12,4},... | collective-permute-start | bytes 110600 | tf_op jit(solution)/shard_map/ppermute | solution.py:33
  16.9 1.9 %collective-permute-start.2 = (bf16[512,1152]{1,0:T(8,128)(2,1)S(1)}, bf16[512,1152]{1,0:T(8,128)(2,1)S(1)}, u32[]{:S(2)}, u32[]{:S(2)}) collective-permute-start(bf16[512,1152]{1,0:T(8,128)(2,1)S(1)} %copy-done), channel_id=1, source_target_pairs={{0,8},{8,0},{1,9},{9,1},{2,10},{10,2},{3,11},{11,3},{4,12},{12,4},... | collective-permute-start | bytes 3538952 | tf_op jit(solution)/shard_map/ppermute | solution.py:33
  18.9 0.6 maximum_select_fusion.moments_ref
  19.6 0.0 all-to-all-done
  19.6 0.1 slice_reduce_fusion
  19.7 6.0 %collective-permute-start.1 = (bf16[64,256]{1,0:T(8,128)(2,1)S(1)}, bf16[64,256]{1,0:T(8,128)(2,1)S(1)}, u32[]{:S(2)}, u32[]{:S(2)}) collective-permute-start(bf16[64,256]{1,0:T(8,128)(2,1)S(1)} %get-tuple-element.28), channel_id=1, source_target_pairs={{0,8},{8,0},{1,9},{9,1},{2,10},{10,2},{3,11},{11,3},{4,12},{12,4},... | collective-permute-start | bytes 98312 | tf_op jit(solution)/shard_map/ppermute | solution.py:33
  25.7 0.1 dynamic-slice_bitcast_fusion.3
  25.8 0.7 collective-permute-done.1
  26.6 13.1 %all_to_all.30.both_ref = bf16[8,80,512]{2,1,0:T(8,128)(2,1)S(1)} all-to-all(bf16[8,80,512]{2,1,0:T(8,128)(2,1)S(1)} %broadcast_in_dim.6), channel_id=1, replica_groups=mesh['y_hi'=2,'z3'=2,'z2'=2,'z1'=2,'z0'=2,'core'=2,'x'=4,'y_lo'=2] {'x',..., dimensions={0} | all-to-all | bytes 1310720 | tf_op jit(solution)/shard_map/all_to_all | solution.py:38
  39.8 0.0 collective-permute-done.2.other_ref
  39.8 1.7 %gradient.1 = bf16[4,8,72,128]{3,2,1,0:T(8,128)(2,1)S(1)} custom-call(bf16[512,1152]{1,0:T(8,128)(2,1)S(1)} %copy-done, bf16[512,1152]{1,0:T(8,128)(2,1)S(1)} %collective-permute-done.2.other_ref, bf16[8,80,512]{2,1,0:T(8,128)(2,1)S(1)} %all_to_all.30.both_ref), custom_call_target="tpu_custom_call" | custom-call | tf_op jit(solution)/shard_map/gradient/pallas_call | solution.py:145
  41.4 12.3 %all_to_all.31 = bf16[4,576,128]{2,1,0:T(8,128)(2,1)S(1)} all-to-all(bf16[4,576,128]{2,1,0:T(8,128)(2,1)S(1)} %bitcast.36), channel_id=1, replica_groups=mesh['y_hi'=2,'z3'=2,'z2'=2,'z1'=2,'z0'=2,'core'=2,'x'=4,'y_lo'=2] {'y_h..., dimensions={0} | all-to-all | bytes 1179648 | tf_op jit(solution)/shard_map/all_to_all | solution.py:219
  53.7 0.1 reduce_sum.25
  53.8 25.6 %all_to_all.32.far_ref = bf16[8,72,128]{2,1,0:T(8,128)(2,1)} all-to-all(bf16[8,72,128]{2,1,0:T(8,128)(2,1)S(1)} %bitcast.40), channel_id=1, replica_groups=mesh['y_hi'=2,'z3'=2,'z2'=2,'z1'=2,'z0'=2,'core'=2,'x'=4,'y_lo'=2] {'z1'..., dimensions={0} | all-to-all | bytes 294912 | tf_op jit(solution)/shard_map/all_to_all | solution.py:220
  79.4 1.7 %step.1 = (bf16[8,72,128]{2,1,0:T(8,128)(2,1)}, f32[2,36,128]{2,1,0:T(8,128)}) custom-call(bf16[8,72,128]{2,1,0:T(8,128)(2,1)} %all_to_all.32.far_ref, f32[2,2,36,128]{3,2,1,0:T(8,128)} %maximum_select_fusion.moments_ref), custom_call_target="tpu_custom_call" | custom-call | tf_op jit(solution)/shard_map/step/pallas_call | solution.py:178
  81.1 4.5 %all-to-all-start.4 = ((bf16[8,72,128]{2,1,0:T(8,128)(2,1)}), bf16[8,72,128]{2,1,0:T(8,128)(2,1)S(1)}, u32[]{:S(2)}, u32[]{:S(2)}) async-start(bf16[8,72,128]{2,1,0:T(8,128)(2,1)} %get-tuple-element.19), calls=%async_computation.4 | async-start | bytes 294912 | tf_op jit(solution)/shard_map/all_to_all | solution.py:222
  85.6 0.8 constant_dynamic-slice_fusion.1
  86.5 6.0 %collective-permute-start.3 = (f32[2,18,128]{2,1,0:T(8,128)S(1)}, f32[2,18,128]{2,1,0:T(8,128)S(1)}, u32[]{:S(2)}, u32[]{:S(2)}) collective-permute-start(f32[2,18,128]{2,1,0:T(8,128)S(1)} %get-tuple-element.32), channel_id=1, source_target_pairs={{0,8},{8,0},{1,9},{9,1},{2,10},{10,2},{3,11},{11,3},{4,12},{12,4},... | collective-permute-start | bytes 55304 | tf_op jit(solution)/shard_map/ppermute | solution.py:33
  92.5 0.8 collective-permute-done.3
  93.3 4.0 %all-to-all-done.4 = bf16[8,72,128]{2,1,0:T(8,128)(2,1)S(1)} async-done(((bf16[8,72,128]{2,1,0:T(8,128)(2,1)}), bf16[8,72,128]{2,1,0:T(8,128)(2,1)S(1)}, u32[]{:S(2)}, u32[]{:S(2)}) %all-to-all-start.4) | async-done | bytes 147488 | tf_op jit(solution)/shard_map/all_to_all | solution.py:222
  97.3 0.1 broadcast_in_dim.15
  97.4 10.4 %all_to_all.33 = bf16[4,576,128]{2,1,0:T(8,128)(2,1)S(1)} all-to-all(bf16[4,576,128]{2,1,0:T(8,128)(2,1)S(1)} %broadcast_in_dim.15), channel_id=1, replica_groups=mesh['y_hi'=2,'z3'=2,'z2'=2,'z1'=2,'z0'=2,'core'=2,'x'=4,'y_lo'=2] {'y_h..., dimensions={0} | all-to-all | bytes 1179648 | tf_op jit(solution)/shard_map/all_to_all | solution.py:38
  107.8 0.5 copy.14
  108.2 0.5 copy.15
  108.7 0.1 copy.23
  108.8 9.0 %collective-permute-start.4 = (bf16[1152,256]{1,0:T(8,128)(2,1)S(1)}, bf16[1152,256]{1,0:T(8,128)(2,1)S(1)}, u32[]{:S(2)}, u32[]{:S(2)}) collective-permute-start(bf16[1152,256]{1,0:T(8,128)(2,1)S(1)} %bitcast.41), channel_id=1, source_target_pairs={{0,8},{8,0},{1,9},{9,1},{2,10},{10,2},{3,11},{11,3},{4,12},{12,4},... | collective-permute-start | bytes 1769480 | tf_op jit(solution)/shard_map/ppermute | solution.py:33
  117.9 0.7 fusion.4
  118.5 0.3 fusion.2
  118.8 0.6 collective-permute-done.4
  119.4 1.0 fusion
  (22 shorter events, 0.2 us)
Async XLA Ops:
  4.3 6.0 %copy-start.1 = (f32[512,18]{0,1:T(8,128)S(1)}, f32[512,18]{0,1:T(8,128)}, u32[]{:S(2)}) copy-start(f32[512,18]{0,1:T(8,128)} %param.9) | copy-start | bytes 110596
  4.3 6.0 %copy-start.2 = (f32[512,18]{0,1:T(8,128)S(1)}, f32[512,18]{0,1:T(8,128)}, u32[]{:S(2)}) copy-start(f32[512,18]{0,1:T(8,128)} %param.8) | copy-start | bytes 110596
  4.3 12.6 %copy-start = (bf16[512,1152]{1,0:T(8,128)(2,1)S(1)}, bf16[512,1152]{1,0:T(8,128)(2,1)}, u32[]{:S(2)}) copy-start(bf16[512,1152]{1,0:T(8,128)(2,1)} %own_ref) | copy-start | bytes 3538948
  4.3 15.3 %all-to-all-start = ((bf16[8,80,512]{2,1,0:T(8,128)(2,1)}), bf16[8,80,512]{2,1,0:T(8,128)(2,1)S(1)}, u32[]{:S(2)}, u32[]{:S(2)}) async-start(bf16[8,80,512]{2,1,0:T(8,128)(2,1)} %project.1), calls=%async_computation | async-start | bytes 1310720 | tf_op jit(solution)/shard_map/all_to_all | solution.py:201
  10.4 8.5 %collective-permute-start = (f32[2,2,18,128]{3,2,1,0:T(8,128)S(1)}, f32[2,2,18,128]{3,2,1,0:T(8,128)S(1)}, u32[]{:S(2)}, u32[]{:S(2)}) collective-permute-start(f32[2,2,18,128]{3,2,1,0:T(8,128)S(1)} %get-tuple-element.26), channel_id=1, source_target_pairs={{0,8},{8,0},{1,9},{9,1},{2,10},{10,2},{3,11},{11,3},{4,12},{12,4},... | collective-permute-start | bytes 110600 | tf_op jit(solution)/shard_map/ppermute | solution.py:33
  16.9 22.8 %collective-permute-start.2 = (bf16[512,1152]{1,0:T(8,128)(2,1)S(1)}, bf16[512,1152]{1,0:T(8,128)(2,1)S(1)}, u32[]{:S(2)}, u32[]{:S(2)}) collective-permute-start(bf16[512,1152]{1,0:T(8,128)(2,1)S(1)} %copy-done), channel_id=1, source_target_pairs={{0,8},{8,0},{1,9},{9,1},{2,10},{10,2},{3,11},{11,3},{4,12},{12,4},... | collective-permute-start | bytes 3538952 | tf_op jit(solution)/shard_map/ppermute | solution.py:33
  19.7 6.9 %collective-permute-start.1 = (bf16[64,256]{1,0:T(8,128)(2,1)S(1)}, bf16[64,256]{1,0:T(8,128)(2,1)S(1)}, u32[]{:S(2)}, u32[]{:S(2)}) collective-permute-start(bf16[64,256]{1,0:T(8,128)(2,1)S(1)} %get-tuple-element.28), channel_id=1, source_target_pairs={{0,8},{8,0},{1,9},{9,1},{2,10},{10,2},{3,11},{11,3},{4,12},{12,4},... | collective-permute-start | bytes 98312 | tf_op jit(solution)/shard_map/ppermute | solution.py:33
  81.1 16.2 %all-to-all-start.4 = ((bf16[8,72,128]{2,1,0:T(8,128)(2,1)}), bf16[8,72,128]{2,1,0:T(8,128)(2,1)S(1)}, u32[]{:S(2)}, u32[]{:S(2)}) async-start(bf16[8,72,128]{2,1,0:T(8,128)(2,1)} %get-tuple-element.19), calls=%async_computation.4 | async-start | bytes 294912 | tf_op jit(solution)/shard_map/all_to_all | solution.py:222
  86.5 6.8 %collective-permute-start.3 = (f32[2,18,128]{2,1,0:T(8,128)S(1)}, f32[2,18,128]{2,1,0:T(8,128)S(1)}, u32[]{:S(2)}, u32[]{:S(2)}) collective-permute-start(f32[2,18,128]{2,1,0:T(8,128)S(1)} %get-tuple-element.32), channel_id=1, source_target_pairs={{0,8},{8,0},{1,9},{9,1},{2,10},{10,2},{3,11},{11,3},{4,12},{12,4},... | collective-permute-start | bytes 55304 | tf_op jit(solution)/shard_map/ppermute | solution.py:33
  108.8 10.6 %collective-permute-start.4 = (bf16[1152,256]{1,0:T(8,128)(2,1)S(1)}, bf16[1152,256]{1,0:T(8,128)(2,1)S(1)}, u32[]{:S(2)}, u32[]{:S(2)}) collective-permute-start(bf16[1152,256]{1,0:T(8,128)(2,1)S(1)} %bitcast.41), channel_id=1, source_target_pairs={{0,8},{8,0},{1,9},{9,1},{2,10},{10,2},{3,11},{11,3},{4,12},{12,4},... | collective-permute-start | bytes 1769480 | tf_op jit(solution)/shard_map/ppermute | solution.py:33

commit v3 on v2

--- a/solution.py
+++ b/solution.py
@@ -109,49 +109,33 @@
 
 
 def gradient_kernel(own_ref, other_ref, both_ref, out_ref, left, total):
-    step = pl.program_id(0)
     few = both_ref.shape[1] - 16
     half = left.shape[2]
-    tokens = own_ref.shape[0]
-    wide = own_ref.shape[1]
-
-    @pl.when(step == 0)
-    def _():
-        for side in range(2):
-            for peer in range(8):
-                left[side, peer * few : (peer + 1) * few, :] = both_ref[
-                    peer, :few, side * half : (side + 1) * half
-                ]
-
-    sums = contract(own_ref[...], left[0], 0, 0) + contract(other_ref[...], left[1], 0, 0)
-    total[pl.ds(pl.multiple_of(step * wide, wide), wide), :] = sums
-
-    @pl.when(step == pl.num_programs(0) - 1)
-    def _():
-        each = out_ref.shape[2] // 2
-        for index in range(total.shape[0] // each):
-            coords = {axis: index >> (4 - bit) & 1 for bit, axis in enumerate(AXES[:5])}
-            block = total[index * each : (index + 1) * each, :]
-            block = jnp.concatenate([block[:, :128], block[:, 128:]], 0)
-            out_ref[place_in(NEAR, coords), place_in(FAR, coords)] = block.astype(bf16)
+    wide = total.shape[0] // 3
+    for side in range(2):
+        for peer in range(8):
+            left[side, peer * few : (peer + 1) * few, :] = both_ref[
+                peer, :few, side * half : (side + 1) * half
+            ]
+    for at in range(0, total.shape[0], wide):
+        sums = contract(own_ref[:, at : at + wide], left[0], 0, 0)
+        total[at : at + wide, :] = sums + contract(other_ref[:, at : at + wide], left[1], 0, 0)
+    each = out_ref.shape[2] // 2
+    for index in range(total.shape[0] // each):
+        coords = {axis: index >> (4 - bit) & 1 for bit, axis in enumerate(AXES[:5])}
+        block = total[index * each : (index + 1) * each, :]
+        block = jnp.concatenate([block[:, :128], block[:, 128:]], 0)
+        out_ref[place_in(NEAR, coords), place_in(FAR, coords)] = block.astype(bf16)
 
 
 def gradient_parts(own, other, both):
     tokens, width = own.shape
     half = both.shape[2] // 2
-    steps = 3
-    wide = width // steps
-    out = (4, 8, width // 16, half // 2)
     return pl.pallas_call(
         gradient_kernel,
-        out_shape=jax.ShapeDtypeStruct(out, bf16),
-        grid=(steps,),
-        in_specs=[
-            pl.BlockSpec((tokens, wide), lambda i: (0, i)),
-            pl.BlockSpec((tokens, wide), lambda i: (0, i)),
-            pl.BlockSpec(both.shape, lambda i: (0, 0, 0)),
-        ],
-        out_specs=pl.BlockSpec(out, lambda i: (0, 0, 0, 0)),
+        out_shape=jax.ShapeDtypeStruct((4, 8, width // 16, half // 2), bf16),
+        in_specs=[pl.BlockSpec(memory_space=pltpu.VMEM)] * 3,
+        out_specs=pl.BlockSpec(memory_space=pltpu.VMEM),
         scratch_shapes=[
             pltpu.VMEM((2, tokens, half), bf16),
             pltpu.VMEM((width, half), f32),
@@ -181,6 +165,7 @@
             jax.ShapeDtypeStruct(far.shape, bf16),
             jax.ShapeDtypeStruct(moments.shape[1:], f32),
         ),
+        in_specs=[pl.BlockSpec(memory_space=pltpu.VMEM)] * 2,
         name="step",
     )(far, moments)
 

time: 121 us -> 120 us (level)
  no operation moved by 1% of the time
where the time goes in v3:
time: 120 us
  blocking collectives  61.4 us (51%)
  starting transfers between devices  40 us (33%)
  Pallas kernels  6.18 us (5%)
  waiting for transfers between devices  6.11 us (5%)
  local copies, waits for them, and re-layouts  2.21 us (2%)
  other arithmetic  1.5 us (1%)
  matrix products  1.34 us (1%)
    ppermute x5, starting transfers between devices, swap_cores(): return lax.ppermute(value, 'core', CORE_SWAP)  29.4 us
    all_to_all x1, blocking collectives, local(): far = lax.all_to_all(near.reshape(8, 2 * each, 128), FAR, 0, 0)  25.6 us
    all_to_all x2, blocking collectives, spread(): return lax.all_to_all(copies, axes, 0, 0)  23.5 us
    all_to_all x1, blocking collectives, local(): near = lax.all_to_all(near, NEAR, 0, 0).astype(f32).sum(0).astype(bf16)  12.2 us
    all_to_all x1, starting transfers between devices, local(): parts = lax.all_to_all(parts, SUMMING, 0, 0)  6 us
    all_to_all x1, starting transfers between devices, local(): normed = lax.all_to_all(normed, FAR, 0, 0)  4.54 us
    all_to_all x1, waiting for transfers between devices, local(): normed = lax.all_to_all(normed, FAR, 0, 0)  3.99 us
    pallas_call x1, Pallas kernels, project(): pl.pallas_call(project_kernel, out_shape=jax.ShapeDtypeStruct((8, few, ra...  3.65 us
  transfers between devices with their start and end apart: 7, of which 4 were waited for; matrix products, arithmetic and copies ran while one was open for 2% of the time, Pallas kernels for 0%

profile of v3, /device:TPU:1, one launch (start us, length us, event | category | flops | bytes accessed | tf_op | source)
XLA Modules:
  0.0 119.6 jit_solution(17747200851870842017)
XLA Ops:
  0.6 3.7 %project.1 = bf16[8,80,512]{2,1,0:T(8,128)(2,1)} custom-call(s32[1]{0:T(128)} %bitcast.start_ref, bf16[512,896]{1,0:T(8,128)(2,1)} %activations_ref.1, f32[896,512]{1,0:T(8,128)} %projector_ref.1), custom_call_target="tpu_custom_call" | custom-call | tf_op jit(solution)/shard_map/project/pallas_call | solution.py:94
  4.3 6.0 %all-to-all-start = ((bf16[8,80,512]{2,1,0:T(8,128)(2,1)}), bf16[8,80,512]{2,1,0:T(8,128)(2,1)S(1)}, u32[]{:S(2)}, u32[]{:S(2)}) async-start(bf16[8,80,512]{2,1,0:T(8,128)(2,1)} %project.1), calls=%async_computation | async-start | bytes 1310720 | tf_op jit(solution)/shard_map/all_to_all | solution.py:186
  10.4 6.5 %collective-permute-start = (f32[2,2,18,128]{3,2,1,0:T(8,128)S(1)}, f32[2,2,18,128]{3,2,1,0:T(8,128)S(1)}, u32[]{:S(2)}, u32[]{:S(2)}) collective-permute-start(f32[2,2,18,128]{3,2,1,0:T(8,128)S(1)} %get-tuple-element.26), channel_id=1, source_target_pairs={{0,8},{8,0},{1,9},{9,1},{2,10},{10,2},{3,11},{11,3},{4,12},{12,4},... | collective-permute-start | bytes 110600 | tf_op jit(solution)/shard_map/ppermute | solution.py:33
  16.9 1.9 %collective-permute-start.2 = (bf16[512,1152]{1,0:T(8,128)(2,1)S(1)}, bf16[512,1152]{1,0:T(8,128)(2,1)S(1)}, u32[]{:S(2)}, u32[]{:S(2)}) collective-permute-start(bf16[512,1152]{1,0:T(8,128)(2,1)S(1)} %copy-done), channel_id=1, source_target_pairs={{0,8},{8,0},{1,9},{9,1},{2,10},{10,2},{3,11},{11,3},{4,12},{12,4},... | collective-permute-start | bytes 3538952 | tf_op jit(solution)/shard_map/ppermute | solution.py:33
  18.9 0.6 maximum_select_fusion.moments_ref
  19.6 0.0 all-to-all-done
  19.6 0.1 slice_reduce_fusion
  19.7 6.0 %collective-permute-start.1 = (bf16[64,256]{1,0:T(8,128)(2,1)S(1)}, bf16[64,256]{1,0:T(8,128)(2,1)S(1)}, u32[]{:S(2)}, u32[]{:S(2)}) collective-permute-start(bf16[64,256]{1,0:T(8,128)(2,1)S(1)} %get-tuple-element.28), channel_id=1, source_target_pairs={{0,8},{8,0},{1,9},{9,1},{2,10},{10,2},{3,11},{11,3},{4,12},{12,4},... | collective-permute-start | bytes 98312 | tf_op jit(solution)/shard_map/ppermute | solution.py:33
  25.7 0.1 dynamic-slice_bitcast_fusion.3
  25.8 0.7 collective-permute-done.1
  26.6 13.1 %all_to_all.30.both_ref = bf16[8,80,512]{2,1,0:T(8,128)(2,1)S(1)} all-to-all(bf16[8,80,512]{2,1,0:T(8,128)(2,1)S(1)} %broadcast_in_dim.6), channel_id=1, replica_groups=mesh['y_hi'=2,'z3'=2,'z2'=2,'z1'=2,'z0'=2,'core'=2,'x'=4,'y_lo'=2] {'x',..., dimensions={0} | all-to-all | bytes 1310720 | tf_op jit(solution)/shard_map/all_to_all | solution.py:38
  39.8 0.0 collective-permute-done.2.other_ref
  39.8 0.9 gradient.1
  40.6 12.2 %all_to_all.31 = bf16[4,576,128]{2,1,0:T(8,128)(2,1)S(1)} all-to-all(bf16[4,576,128]{2,1,0:T(8,128)(2,1)S(1)} %bitcast.36), channel_id=1, replica_groups=mesh['y_hi'=2,'z3'=2,'z2'=2,'z1'=2,'z0'=2,'core'=2,'x'=4,'y_lo'=2] {'y_h..., dimensions={0} | all-to-all | bytes 1179648 | tf_op jit(solution)/shard_map/all_to_all | solution.py:204
  52.9 0.1 reduce_sum.25
  53.0 25.6 %all_to_all.32.far_ref = bf16[8,72,128]{2,1,0:T(8,128)(2,1)} all-to-all(bf16[8,72,128]{2,1,0:T(8,128)(2,1)S(1)} %bitcast.40), channel_id=1, replica_groups=mesh['y_hi'=2,'z3'=2,'z2'=2,'z1'=2,'z0'=2,'core'=2,'x'=4,'y_lo'=2] {'z1'..., dimensions={0} | all-to-all | bytes 294912 | tf_op jit(solution)/shard_map/all_to_all | solution.py:205
  78.6 1.7 %step.1 = (bf16[8,72,128]{2,1,0:T(8,128)(2,1)}, f32[2,36,128]{2,1,0:T(8,128)}) custom-call(bf16[8,72,128]{2,1,0:T(8,128)(2,1)} %all_to_all.32.far_ref, f32[2,2,36,128]{3,2,1,0:T(8,128)} %maximum_select_fusion.moments_ref), custom_call_target="tpu_custom_call" | custom-call | tf_op jit(solution)/shard_map/step/pallas_call | solution.py:162
  80.3 4.5 %all-to-all-start.4 = ((bf16[8,72,128]{2,1,0:T(8,128)(2,1)}), bf16[8,72,128]{2,1,0:T(8,128)(2,1)S(1)}, u32[]{:S(2)}, u32[]{:S(2)}) async-start(bf16[8,72,128]{2,1,0:T(8,128)(2,1)} %get-tuple-element.19), calls=%async_computation.4 | async-start | bytes 294912 | tf_op jit(solution)/shard_map/all_to_all | solution.py:207
  84.8 0.8 constant_dynamic-slice_fusion.1
  85.7 6.0 %collective-permute-start.3 = (f32[2,18,128]{2,1,0:T(8,128)S(1)}, f32[2,18,128]{2,1,0:T(8,128)S(1)}, u32[]{:S(2)}, u32[]{:S(2)}) collective-permute-start(f32[2,18,128]{2,1,0:T(8,128)S(1)} %get-tuple-element.32), channel_id=1, source_target_pairs={{0,8},{8,0},{1,9},{9,1},{2,10},{10,2},{3,11},{11,3},{4,12},{12,4},... | collective-permute-start | bytes 55304 | tf_op jit(solution)/shard_map/ppermute | solution.py:33
  91.6 0.8 collective-permute-done.3
  92.5 4.0 %all-to-all-done.4 = bf16[8,72,128]{2,1,0:T(8,128)(2,1)S(1)} async-done(((bf16[8,72,128]{2,1,0:T(8,128)(2,1)}), bf16[8,72,128]{2,1,0:T(8,128)(2,1)S(1)}, u32[]{:S(2)}, u32[]{:S(2)}) %all-to-all-start.4) | async-done | bytes 147488 | tf_op jit(solution)/shard_map/all_to_all | solution.py:207
  96.5 0.1 broadcast_in_dim.15
  96.6 10.4 %all_to_all.33 = bf16[4,576,128]{2,1,0:T(8,128)(2,1)S(1)} all-to-all(bf16[4,576,128]{2,1,0:T(8,128)(2,1)S(1)} %broadcast_in_dim.15), channel_id=1, replica_groups=mesh['y_hi'=2,'z3'=2,'z2'=2,'z1'=2,'z0'=2,'core'=2,'x'=4,'y_lo'=2] {'y_h..., dimensions={0} | all-to-all | bytes 1179648 | tf_op jit(solution)/shard_map/all_to_all | solution.py:38
  106.9 0.5 copy.14
  107.4 0.5 copy.15
  107.9 0.1 copy.23
  108.0 9.0 %collective-permute-start.4 = (bf16[1152,256]{1,0:T(8,128)(2,1)S(1)}, bf16[1152,256]{1,0:T(8,128)(2,1)S(1)}, u32[]{:S(2)}, u32[]{:S(2)}) collective-permute-start(bf16[1152,256]{1,0:T(8,128)(2,1)S(1)} %bitcast.41), channel_id=1, source_target_pairs={{0,8},{8,0},{1,9},{9,1},{2,10},{10,2},{3,11},{11,3},{4,12},{12,4},... | collective-permute-start | bytes 1769480 | tf_op jit(solution)/shard_map/ppermute | solution.py:33
  117.0 0.7 fusion.4
  117.7 0.3 fusion.2
  118.0 0.6 collective-permute-done.4
  118.6 1.0 fusion
  (22 shorter events, 0.2 us)
Async XLA Ops:
  4.3 6.0 %copy-start.1 = (f32[512,18]{0,1:T(8,128)S(1)}, f32[512,18]{0,1:T(8,128)}, u32[]{:S(2)}) copy-start(f32[512,18]{0,1:T(8,128)} %param.9) | copy-start | bytes 110596
  4.3 6.0 %copy-start.2 = (f32[512,18]{0,1:T(8,128)S(1)}, f32[512,18]{0,1:T(8,128)}, u32[]{:S(2)}) copy-start(f32[512,18]{0,1:T(8,128)} %param.8) | copy-start | bytes 110596
  4.3 12.6 %copy-start = (bf16[512,1152]{1,0:T(8,128)(2,1)S(1)}, bf16[512,1152]{1,0:T(8,128)(2,1)}, u32[]{:S(2)}) copy-start(bf16[512,1152]{1,0:T(8,128)(2,1)} %own_ref) | copy-start | bytes 3538948
  4.3 15.3 %all-to-all-start = ((bf16[8,80,512]{2,1,0:T(8,128)(2,1)}), bf16[8,80,512]{2,1,0:T(8,128)(2,1)S(1)}, u32[]{:S(2)}, u32[]{:S(2)}) async-start(bf16[8,80,512]{2,1,0:T(8,128)(2,1)} %project.1), calls=%async_computation | async-start | bytes 1310720 | tf_op jit(solution)/shard_map/all_to_all | solution.py:186
  10.4 8.5 %collective-permute-start = (f32[2,2,18,128]{3,2,1,0:T(8,128)S(1)}, f32[2,2,18,128]{3,2,1,0:T(8,128)S(1)}, u32[]{:S(2)}, u32[]{:S(2)}) collective-permute-start(f32[2,2,18,128]{3,2,1,0:T(8,128)S(1)} %get-tuple-element.26), channel_id=1, source_target_pairs={{0,8},{8,0},{1,9},{9,1},{2,10},{10,2},{3,11},{11,3},{4,12},{12,4},... | collective-permute-start | bytes 110600 | tf_op jit(solution)/shard_map/ppermute | solution.py:33
  16.9 22.8 %collective-permute-start.2 = (bf16[512,1152]{1,0:T(8,128)(2,1)S(1)}, bf16[512,1152]{1,0:T(8,128)(2,1)S(1)}, u32[]{:S(2)}, u32[]{:S(2)}) collective-permute-start(bf16[512,1152]{1,0:T(8,128)(2,1)S(1)} %copy-done), channel_id=1, source_target_pairs={{0,8},{8,0},{1,9},{9,1},{2,10},{10,2},{3,11},{11,3},{4,12},{12,4},... | collective-permute-start | bytes 3538952 | tf_op jit(solution)/shard_map/ppermute | solution.py:33
  19.7 6.9 %collective-permute-start.1 = (bf16[64,256]{1,0:T(8,128)(2,1)S(1)}, bf16[64,256]{1,0:T(8,128)(2,1)S(1)}, u32[]{:S(2)}, u32[]{:S(2)}) collective-permute-start(bf16[64,256]{1,0:T(8,128)(2,1)S(1)} %get-tuple-element.28), channel_id=1, source_target_pairs={{0,8},{8,0},{1,9},{9,1},{2,10},{10,2},{3,11},{11,3},{4,12},{12,4},... | collective-permute-start | bytes 98312 | tf_op jit(solution)/shard_map/ppermute | solution.py:33
  80.3 16.2 %all-to-all-start.4 = ((bf16[8,72,128]{2,1,0:T(8,128)(2,1)}), bf16[8,72,128]{2,1,0:T(8,128)(2,1)S(1)}, u32[]{:S(2)}, u32[]{:S(2)}) async-start(bf16[8,72,128]{2,1,0:T(8,128)(2,1)} %get-tuple-element.19), calls=%async_computation.4 | async-start | bytes 294912 | tf_op jit(solution)/shard_map/all_to_all | solution.py:207
  85.7 6.8 %collective-permute-start.3 = (f32[2,18,128]{2,1,0:T(8,128)S(1)}, f32[2,18,128]{2,1,0:T(8,128)S(1)}, u32[]{:S(2)}, u32[]{:S(2)}) collective-permute-start(f32[2,18,128]{2,1,0:T(8,128)S(1)} %get-tuple-element.32), channel_id=1, source_target_pairs={{0,8},{8,0},{1,9},{9,1},{2,10},{10,2},{3,11},{11,3},{4,12},{12,4},... | collective-permute-start | bytes 55304 | tf_op jit(solution)/shard_map/ppermute | solution.py:33
  108.0 10.6 %collective-permute-start.4 = (bf16[1152,256]{1,0:T(8,128)(2,1)S(1)}, bf16[1152,256]{1,0:T(8,128)(2,1)S(1)}, u32[]{:S(2)}, u32[]{:S(2)}) collective-permute-start(bf16[1152,256]{1,0:T(8,128)(2,1)S(1)} %bitcast.41), channel_id=1, source_target_pairs={{0,8},{8,0},{1,9},{9,1},{2,10},{10,2},{3,11},{11,3},{4,12},{12,4},... | collective-permute-start | bytes 1769480 | tf_op jit(solution)/shard_map/ppermute | solution.py:33

commit v4 on v3

v4 whole, which is shorter than its diff:
```python
import jax
import jax.numpy as jnp
from jax import lax
from jax.experimental import pallas as pl
from jax.experimental.pallas import tpu as pltpu
from jax.sharding import Mesh, PartitionSpec as P

beta_first = 0.9
beta_second = 0.999
bias_first = 0.999973438601112
bias_second = 0.095207852886291
adam_eps = 1e-08

AXES = ("y_hi", "z3", "z2", "z1", "z0", "core", "x", "y_lo")
SIZES = (2, 2, 2, 2, 2, 2, 4, 2)
DP = AXES[:6]
TENSOR = AXES[6:]
GATHERING = ("x", "y_lo")
SUMMING = ("x", "y_lo", "core")
NEAR = ("y_hi", "z0")
FAR = ("z1", "z2", "z3")
bf16, f32 = jnp.bfloat16, jnp.float32
CORE_SWAP = [(0, 1), (1, 0)]


def place_in(axes, coords):
    index = 0
    for axis in axes:
        index = index * SIZES[AXES.index(axis)] + coords[axis]
    return index


def swap_cores(value):
    return lax.ppermute(value, "core", CORE_SWAP)


def spread(value, axes, count):
    copies = jnp.broadcast_to(value[None], (count,) + value.shape)
    return lax.all_to_all(copies, axes, 0, 0)


def halves(value, core, axis):
    first, second = jnp.split(value, 2, axis)
    return jnp.where(core == 0, first, second), jnp.where(core == 0, second, first)


def in_order(own, other, place, axis):
    return jnp.where(
        place == 0,
        jnp.concatenate([own, other], axis),
        jnp.concatenate([other, own], axis),
    )


def adam(decayed_one, decayed_two, gradient):
    first = decayed_one + (1.0 - beta_first) * gradient
    second = decayed_two + (1.0 - beta_second) * gradient * gradient
    return first, second


def in_two(value):
    high = value.astype(bf16)
    return high, (value - high.astype(f32)).astype(bf16)


def contract(left, right, left_dim, right_dim):
    return lax.dot_general(
        left, right, (((left_dim,), (right_dim,)), ((), ())), preferred_element_type=f32
    )


def project_kernel(place_ref, activations_ref, projector_ref, parts_ref):
    high, low = in_two(projector_ref[...])
    left = activations_ref[...]
    sums = (contract(left, high, 1, 0) + contract(left, low, 1, 0)).astype(bf16)
    few = left.shape[0] // 8
    rows = projector_ref.shape[0] // 8
    for peer in range(8):
        parts_ref[peer, :few, :] = sums[peer * few : (peer + 1) * few]
        eighth = jnp.minimum(peer * 2 + place_ref[0] % 2, rows // 8 - 1) * 8
        start = place_ref[0] // 2 * (2 * rows) + eighth
        basis = [
            projector_ref[pl.ds(pl.multiple_of(start + side * rows, 8), 8), :] for side in range(2)
        ]
        parts_ref[peer, few:, :] = jnp.concatenate(basis, 0).astype(bf16)


def project(activations, projector, place):
    tokens, features = activations.shape
    half = projector.shape[1] // 2
    few = tokens // 8 + 16
    return pl.pallas_call(
        project_kernel,
        out_shape=jax.ShapeDtypeStruct((8, 2 * few, half), bf16),
        grid_spec=pltpu.PrefetchScalarGridSpec(
            num_scalar_prefetch=1,
            grid=(2,),
            in_specs=[
                pl.BlockSpec((tokens, features), lambda i, _: (0, 0)),
                pl.BlockSpec((features, half), lambda i, _: (0, i)),
            ],
            out_specs=pl.BlockSpec((8, few, half), lambda i, _: (0, i, 0)),
        ),
        compiler_params=pltpu.CompilerParams(vmem_limit_bytes=58 << 20),
        name="project",
    )(place.reshape(1).astype(jnp.int32), activations, projector)


def gradient_kernel(core_ref, own_ref, other_ref, both_ref, out_ref, left, total):
    full = both_ref.shape[1] // 2
    few = full - 16
    wide = total.shape[0] // 3
    for side in range(2):
        for peer in range(8):
            left[side, peer * few : (peer + 1) * few, :] = both_ref[
                peer, side * full : side * full + few, :
            ]
    core = core_ref[0]
    for at in range(0, total.shape[0], wide):
        sums = contract(own_ref[:, at : at + wide], left[core], 0, 0)
        total[at : at + wide, :] = sums + contract(other_ref[:, at : at + wide], left[1 - core], 0, 0)
    each = out_ref.shape[2] // 2
    for index in range(total.shape[0] // each):
        coords = {axis: index >> (4 - bit) & 1 for bit, axis in enumerate(AXES[:5])}
        block = total[index * each : (index + 1) * each, :]
        block = jnp.concatenate([block[:, :128], block[:, 128:]], 0)
        out_ref[place_in(NEAR, coords), place_in(FAR, coords)] = block.astype(bf16)


def gradient_parts(own, other, both, core):
    tokens, width = own.shape
    half = both.shape[2]
    return pl.pallas_call(
        gradient_kernel,
        out_shape=jax.ShapeDtypeStruct((4, 8, width // 16, half // 2), bf16),
        in_specs=[pl.BlockSpec(memory_space=pltpu.SMEM)]
        + [pl.BlockSpec(memory_space=pltpu.VMEM)] * 3,
        out_specs=pl.BlockSpec(memory_space=pltpu.VMEM),
        scratch_shapes=[
            pltpu.VMEM((2, tokens, half), bf16),
            pltpu.VMEM((width, half), f32),
        ],
        compiler_params=pltpu.CompilerParams(vmem_limit_bytes=40 << 20),
        name="gradient",
    )(core.reshape(1).astype(jnp.int32), own, other, both)


def step_kernel(far_ref, moments_ref, normed_ref, total_ref):
    total = jnp.sum(far_ref[...].astype(f32), axis=0)
    each = total.shape[0] // 2
    for part in range(2):
        total_ref[part] = total[part * each : (part + 1) * each]
    decayed = [jnp.concatenate([moments_ref[i, 0], moments_ref[i, 1]], 0) for i in range(2)]
    first, second = adam(decayed[0], decayed[1], total)
    normed = first / bias_first / (jnp.sqrt(second / bias_second) + adam_eps)
    normed = normed.astype(bf16)
    for place in range(8):
        normed_ref[place] = normed


def step(far, moments):
    return pl.pallas_call(
        step_kernel,
        out_shape=(
            jax.ShapeDtypeStruct(far.shape, bf16),
            jax.ShapeDtypeStruct(moments.shape[1:], f32),
        ),
        in_specs=[pl.BlockSpec(memory_space=pltpu.VMEM)] * 2,
        compiler_params=pltpu.CompilerParams(vmem_limit_bytes=16 << 20),
        name="step",
    )(far, moments)


def local(activations, out_grad, projector, moment_one, moment_two):
    y_hi, z3, z2, z1, z0, core = (lax.axis_index(axis) for axis in DP)
    tokens, rank, width = out_grad.shape[0], projector.shape[1], out_grad.shape[1]
    half = rank // 2
    each = width // 32
    few = tokens // 8
    rows = projector.shape[0] // 8

    parts = project(activations, projector, z1 * 4 + z0 * 2 + core)
    parts, out_grad, moment_one, moment_two = lax.optimization_barrier(
        (parts, out_grad, moment_one, moment_two)
    )
    parts = lax.all_to_all(parts.reshape(16, few + 16, half), SUMMING, 0, 0)
    parts = parts.reshape(8, 2, few + 16, half)

    grad_other = swap_cores(out_grad)
    moments = jnp.stack([beta_first * moment_one.T, beta_second * moment_two.T])
    keep, send = halves(moments.reshape(2, each // 2, 4, 128).transpose(0, 2, 1, 3), core, 1)
    moments = in_order(keep, swap_cores(send), core, 2)

    summed = parts[:, :, :few].astype(f32).sum(0).astype(bf16)
    holder = place_in(GATHERING, {"x": y_hi * 2 + z3, "y_lo": z2})
    basis = lax.dynamic_index_in_dim(parts[:, :, few:], holder, 0, keepdims=False)
    summed, moments = lax.optimization_barrier((summed, moments))
    both = jnp.concatenate([summed, basis], 1).reshape(2 * few + 32, half)
    both = spread(both, GATHERING, 8)

    near = gradient_parts(out_grad, grad_other, both, core).reshape(4, 16 * each, 128)
    near = lax.all_to_all(near, NEAR, 0, 0).astype(f32).sum(0).astype(bf16)
    far = lax.all_to_all(near.reshape(8, 2 * each, 128), FAR, 0, 0)
    normed, total = step(far, moments)
    normed = lax.all_to_all(normed, FAR, 0, 0)

    total, both = lax.optimization_barrier((total, both))
    basis = both.reshape(16, few + 16, half)[: rows // 8, few:].reshape(rows // 8, 2, 8, half)
    basis = basis.transpose(1, 0, 2, 3).reshape(2, rows, half)
    back_own, back_other = halves(total, core, 1)
    own_gradient = in_order(back_own, swap_cores(back_other), core, 0)
    basis = halves(basis, core, 0)
    normed, own_gradient, basis = lax.optimization_barrier((normed, own_gradient, basis))
    own_gradient = own_gradient.transpose(1, 0, 2).reshape(each // 2, rank).T
    moment_first, moment_second = adam(
        beta_first * moment_one, beta_second * moment_two, own_gradient
    )

    normed = spread(normed.reshape(16 * each, 128), NEAR, 4)
    normed = normed.reshape((2,) * 6 + (each, 128))
    order = [(NEAR + FAR).index(axis) for axis in AXES[:5]]
    normed = normed.transpose(*order, 6, 5, 7).reshape(width, half)
    basis_own, basis_other = basis
    update_other = swap_cores(contract(basis_other[0], normed, 1, 1).astype(bf16))
    update = contract(basis_own[0], normed, 1, 1) + update_other.astype(f32)
    return (update.astype(bf16), moment_first, moment_second)


def solution(mesh):
    fine = Mesh(mesh.devices.reshape(SIZES), AXES)
    placed = (
        P(DP, TENSOR),
        P(DP, TENSOR),
        P(TENSOR, None),
        P(None, TENSOR + DP),
        P(None, TENSOR + DP),
    )
    return jax.shard_map(
        local,
        mesh=fine,
        in_specs=placed,
        out_specs=(P(DP, TENSOR), P(None, TENSOR + DP), P(None, TENSOR + DP)),
        check_vma=False,
    )
```

time: 120 us -> 117 us (0.975)
  blocking collectives: 61.4 us -> 45.9 us
  waiting for transfers between devices: 6.11 us -> 21.2 us
    all_to_all x1 -> x2, waiting for transfers between devices: 0.01 us -> 15 us  [the longest x1 9.49 us: spread(): return lax.all_to_all(copies, axes, 0, 0)]
    all_to_all x2 -> x1, blocking collectives: 23.5 us -> 10.7 us  [spread(): return lax.all_to_all(copies, axes, 0, 0)]
    ppermute x5 -> x4, starting transfers between devices: 29.4 us -> 20.5 us  [swap_cores(): return lax.ppermute(value, 'core', CORE_SWAP)]
    all_to_all x1 -> x2, starting transfers between devices: 6 us -> 13.9 us  [the longest x1 10.4 us: local(): parts = lax.all_to_all(parts.reshape(16, few + 16, half), SUMMING, 0, 0)]
    all_to_all x1, blocking collectives: 12.2 us -> 10.9 us  [local(): near = lax.all_to_all(near, NEAR, 0, 0).astype(f32).sum(0).astype(bf16)]
    all_to_all x1, blocking collectives: 25.6 us -> 24.3 us  [local(): far = lax.all_to_all(near.reshape(8, 2 * each, 128), FAR, 0, 0)]
  transfers between devices with their start and end apart: 7 -> 7, of which waited for: 4 -> 6; matrix products, arithmetic and copies ran while one was open for 2% -> 2% of each run, Pallas kernels for 0% -> 0%
where the time goes in v4:
time: 117 us; the launch traced here: 116 us
  blocking collectives  45.9 us (39%)
  starting transfers between devices  39 us (33%)
  waiting for transfers between devices  21.2 us (18%)
  Pallas kernels  5.26 us (4%)
  local copies, waits for them, and re-layouts  2 us (2%)
  matrix products  1.34 us (1%)
    all_to_all x1, blocking collectives, local(): far = lax.all_to_all(near.reshape(8, 2 * each, 128), FAR, 0, 0)  24.3 us
    ppermute x4, starting transfers between devices, swap_cores(): return lax.ppermute(value, 'core', CORE_SWAP)  20.5 us
    all_to_all x1, blocking collectives, local(): near = lax.all_to_all(near, NEAR, 0, 0).astype(f32).sum(0).astype(bf16)  10.9 us
    all_to_all x1, blocking collectives, spread(): return lax.all_to_all(copies, axes, 0, 0)  10.7 us
    all_to_all x1, starting transfers between devices, local(): parts = lax.all_to_all(parts.reshape(16, few + 16, half), SUMMING, 0, 0)  10.4 us
    all_to_all x1, waiting for transfers between devices, spread(): return lax.all_to_all(copies, axes, 0, 0)  9.49 us
    all_to_all x1, waiting for transfers between devices, local(): parts = lax.all_to_all(parts.reshape(16, few + 16, half), SUMMING, 0, 0)  5.48 us
    all_to_all x1, starting transfers between devices, local(): normed = lax.all_to_all(normed, FAR, 0, 0)  4.54 us
  transfers between devices with their start and end apart: 7, of which 6 were waited for; matrix products, arithmetic and copies ran while one was open for 2% of the time, Pallas kernels for 0%

profile of v4, /device:TPU:1, one launch (start us, length us, event | category | flops | bytes accessed | tf_op | source)
XLA Modules:
  0.0 116.4 jit_solution(5647897728739953962)
XLA Ops:
  0.6 3.7 %project.1 = bf16[8,160,256]{2,1,0:T(8,128)(2,1)} custom-call(s32[1]{0:T(128)} %bitcast.1.place_ref, bf16[512,896]{1,0:T(8,128)(2,1)} %activations_ref.1, f32[896,512]{1,0:T(8,128)} %projector_ref.1), custom_call_target="tpu_custom_call" | custom-call | tf_op jit(solution)/shard_map/project/pallas_call | solution.py:92
  4.3 10.4 %all-to-all-start = ((bf16[16,80,256]{2,1,0:T(8,128)(2,1)}), bf16[16,80,256]{2,1,0:T(8,128)(2,1)S(1)}, u32[]{:S(2)}, u32[]{:S(2)}) async-start(bf16[16,80,256]{2,1,0:T(8,128)(2,1)} %bitcast.60), calls=%async_computation | async-start | bytes 1310720 | tf_op jit(solution)/shard_map/all_to_all | solution.py:186
  14.7 0.0 copy-done
  14.7 2.1 %collective-permute-start = (bf16[512,1152]{1,0:T(8,128)(2,1)S(1)}, bf16[512,1152]{1,0:T(8,128)(2,1)S(1)}, u32[]{:S(2)}, u32[]{:S(2)}) collective-permute-start(bf16[512,1152]{1,0:T(8,128)(2,1)S(1)} %copy-done), channel_id=1, source_target_pairs={{0,8},{8,0},{1,9},{9,1},{2,10},{10,2},{3,11},{11,3},{4,12},{12,4},... | collective-permute-start | bytes 3538952 | tf_op jit(solution)/shard_map/ppermute | solution.py:34
  16.9 0.0 copy-done.1
  16.9 0.0 copy-done.2
  17.0 2.2 %collective-permute-start.1 = (f32[2,2,18,128]{3,2,1,0:T(8,128)S(1)}, f32[2,2,18,128]{3,2,1,0:T(8,128)S(1)}, u32[]{:S(2)}, u32[]{:S(2)}) collective-permute-start(f32[2,2,18,128]{3,2,1,0:T(8,128)S(1)} %get-tuple-element.34), channel_id=1, source_target_pairs={{0,8},{8,0},{1,9},{9,1},{2,10},{10,2},{3,11},{11,3},{4,12},{12,4},... | collective-permute-start | bytes 110600 | tf_op jit(solution)/shard_map/ppermute | solution.py:34
  19.2 0.9 collective-permute-done.1
  20.2 5.5 %all-to-all-done = bf16[16,80,256]{2,1,0:T(8,128)(2,1)S(1)} async-done(((bf16[16,80,256]{2,1,0:T(8,128)(2,1)}), bf16[16,80,256]{2,1,0:T(8,128)(2,1)S(1)}, u32[]{:S(2)}, u32[]{:S(2)}) %all-to-all-start) | async-done | bytes 655392 | tf_op jit(solution)/shard_map/all_to_all | solution.py:186
  25.7 0.1 slice_reduce_fusion
  25.8 0.9 broadcast_in_dim.15
  26.7 3.5 %all-to-all-start.1 = ((bf16[8,160,256]{2,1,0:T(8,128)(2,1)}), bf16[8,160,256]{2,1,0:T(8,128)(2,1)S(1)}, u32[]{:S(2)}, u32[]{:S(2)}) async-start(bf16[8,160,256]{2,1,0:T(8,128)(2,1)} %broadcast_in_dim.15), calls=%async_computation.1 | async-start | bytes 1310720 | tf_op jit(solution)/shard_map/all_to_all | solution.py:39
  30.2 0.0 collective-permute-done.other_ref
  30.2 9.5 %all-to-all-done.1.both_ref = bf16[8,160,256]{2,1,0:T(8,128)(2,1)S(1)} async-done(((bf16[8,160,256]{2,1,0:T(8,128)(2,1)}), bf16[8,160,256]{2,1,0:T(8,128)(2,1)S(1)}, u32[]{:S(2)}, u32[]{:S(2)}) %all-to-all-start.1) | async-done | bytes 655392 | tf_op jit(solution)/shard_map/all_to_all | solution.py:39
  39.7 0.9 gradient.1
  40.6 10.9 %all_to_all.30 = bf16[4,576,128]{2,1,0:T(8,128)(2,1)S(1)} all-to-all(bf16[4,576,128]{2,1,0:T(8,128)(2,1)S(1)} %bitcast.55), channel_id=1, replica_groups=mesh['y_hi'=2,'z3'=2,'z2'=2,'z1'=2,'z0'=2,'core'=2,'x'=4,'y_lo'=2] {'y_h..., dimensions={0} | all-to-all | bytes 1179648 | tf_op jit(solution)/shard_map/all_to_all | solution.py:202
  51.5 0.1 reduce_sum.25
  51.5 24.3 %all_to_all.31.far_ref = bf16[8,72,128]{2,1,0:T(8,128)(2,1)S(1)} all-to-all(bf16[8,72,128]{2,1,0:T(8,128)(2,1)S(1)} %bitcast.62), channel_id=1, replica_groups=mesh['y_hi'=2,'z3'=2,'z2'=2,'z1'=2,'z0'=2,'core'=2,'x'=4,'y_lo'=2] {'z1'..., dimensions={0} | all-to-all | bytes 294912 | tf_op jit(solution)/shard_map/all_to_all | solution.py:203
  75.9 0.7 step.1
  76.6 4.5 %all-to-all-start.4 = ((bf16[8,72,128]{2,1,0:T(8,128)(2,1)}), bf16[8,72,128]{2,1,0:T(8,128)(2,1)S(1)}, u32[]{:S(2)}, u32[]{:S(2)}) async-start(bf16[8,72,128]{2,1,0:T(8,128)(2,1)} %get-tuple-element.23), calls=%async_computation.4 | async-start | bytes 294912 | tf_op jit(solution)/shard_map/all_to_all | solution.py:205
  81.2 6.8 %collective-permute-start.2 = (f32[2,18,128]{2,1,0:T(8,128)S(1)}, f32[2,18,128]{2,1,0:T(8,128)S(1)}, u32[]{:S(2)}, u32[]{:S(2)}) collective-permute-start(f32[2,18,128]{2,1,0:T(8,128)S(1)} %get-tuple-element.38), channel_id=1, source_target_pairs={{0,8},{8,0},{1,9},{9,1},{2,10},{10,2},{3,11},{11,3},{4,12},{12,4},... | collective-permute-start | bytes 55304 | tf_op jit(solution)/shard_map/ppermute | solution.py:34
  88.0 0.8 collective-permute-done.2
  88.7 4.1 %all-to-all-done.4 = bf16[8,72,128]{2,1,0:T(8,128)(2,1)S(1)} async-done(((bf16[8,72,128]{2,1,0:T(8,128)(2,1)}), bf16[8,72,128]{2,1,0:T(8,128)(2,1)S(1)}, u32[]{:S(2)}, u32[]{:S(2)}) %all-to-all-start.4) | async-done | bytes 147488 | tf_op jit(solution)/shard_map/all_to_all | solution.py:205
  92.8 0.1 broadcast_in_dim.17
  92.9 10.7 %all_to_all.32 = bf16[4,576,128]{2,1,0:T(8,128)(2,1)S(1)} all-to-all(bf16[4,576,128]{2,1,0:T(8,128)(2,1)S(1)} %broadcast_in_dim.17), channel_id=1, replica_groups=mesh['y_hi'=2,'z3'=2,'z2'=2,'z1'=2,'z0'=2,'core'=2,'x'=4,'y_lo'=2] {'y_h..., dimensions={0} | all-to-all | bytes 1179648 | tf_op jit(solution)/shard_map/all_to_all | solution.py:39
  103.5 0.5 copy.14
  104.0 0.5 copy.15
  104.5 0.3 convolution_convert_fusion
  104.8 9.5 %collective-permute-start.3 = (bf16[112,1152]{1,0:T(8,128)(2,1)S(1)}, bf16[112,1152]{1,0:T(8,128)(2,1)S(1)}, u32[]{:S(2)}, u32[]{:S(2)}) collective-permute-start(bf16[112,1152]{1,0:T(8,128)(2,1)S(1)} %convolution_convert_fusion), channel_id=1, source_target_pairs={{0,8},{8,0},{1,9},{9,1},{2,10},{10,2},{3,11},{11,3},{4,12},{12,4},... | collective-permute-start | bytes 774152 | tf_op jit(solution)/shard_map/ppermute | solution.py:34
  114.3 0.7 fusion.11
  115.0 0.4 collective-permute-done.3
  115.4 1.0 add_convert_fusion
  (21 shorter events, 0.2 us)
Async XLA Ops:
  4.3 10.4 %copy-start = (bf16[512,1152]{1,0:T(8,128)(2,1)S(1)}, bf16[512,1152]{1,0:T(8,128)(2,1)}, u32[]{:S(2)}) copy-start(bf16[512,1152]{1,0:T(8,128)(2,1)} %own_ref) | copy-start | bytes 3538948
  4.3 12.5 %copy-start.1 = (f32[512,18]{0,1:T(8,128)S(1)}, f32[512,18]{0,1:T(8,128)}, u32[]{:S(2)}) copy-start(f32[512,18]{0,1:T(8,128)} %param.9) | copy-start | bytes 110596
  4.3 12.6 %copy-start.2 = (f32[512,18]{0,1:T(8,128)S(1)}, f32[512,18]{0,1:T(8,128)}, u32[]{:S(2)}) copy-start(f32[512,18]{0,1:T(8,128)} %param.8) | copy-start | bytes 110596
  4.3 21.3 %all-to-all-start = ((bf16[16,80,256]{2,1,0:T(8,128)(2,1)}), bf16[16,80,256]{2,1,0:T(8,128)(2,1)S(1)}, u32[]{:S(2)}, u32[]{:S(2)}) async-start(bf16[16,80,256]{2,1,0:T(8,128)(2,1)} %bitcast.60), calls=%async_computation | async-start | bytes 1310720 | tf_op jit(solution)/shard_map/all_to_all | solution.py:186
  14.7 15.5 %collective-permute-start = (bf16[512,1152]{1,0:T(8,128)(2,1)S(1)}, bf16[512,1152]{1,0:T(8,128)(2,1)S(1)}, u32[]{:S(2)}, u32[]{:S(2)}) collective-permute-start(bf16[512,1152]{1,0:T(8,128)(2,1)S(1)} %copy-done), channel_id=1, source_target_pairs={{0,8},{8,0},{1,9},{9,1},{2,10},{10,2},{3,11},{11,3},{4,12},{12,4},... | collective-permute-start | bytes 3538952 | tf_op jit(solution)/shard_map/ppermute | solution.py:34
  17.0 3.1 %collective-permute-start.1 = (f32[2,2,18,128]{3,2,1,0:T(8,128)S(1)}, f32[2,2,18,128]{3,2,1,0:T(8,128)S(1)}, u32[]{:S(2)}, u32[]{:S(2)}) collective-permute-start(f32[2,2,18,128]{3,2,1,0:T(8,128)S(1)} %get-tuple-element.34), channel_id=1, source_target_pairs={{0,8},{8,0},{1,9},{9,1},{2,10},{10,2},{3,11},{11,3},{4,12},{12,4},... | collective-permute-start | bytes 110600 | tf_op jit(solution)/shard_map/ppermute | solution.py:34
  26.7 13.0 %all-to-all-start.1 = ((bf16[8,160,256]{2,1,0:T(8,128)(2,1)}), bf16[8,160,256]{2,1,0:T(8,128)(2,1)S(1)}, u32[]{:S(2)}, u32[]{:S(2)}) async-start(bf16[8,160,256]{2,1,0:T(8,128)(2,1)} %broadcast_in_dim.15), calls=%async_computation.1 | async-start | bytes 1310720 | tf_op jit(solution)/shard_map/all_to_all | solution.py:39
  76.6 16.2 %all-to-all-start.4 = ((bf16[8,72,128]{2,1,0:T(8,128)(2,1)}), bf16[8,72,128]{2,1,0:T(8,128)(2,1)S(1)}, u32[]{:S(2)}, u32[]{:S(2)}) async-start(bf16[8,72,128]{2,1,0:T(8,128)(2,1)} %get-tuple-element.23), calls=%async_computation.4 | async-start | bytes 294912 | tf_op jit(solution)/shard_map/all_to_all | solution.py:205
  81.2 7.6 %collective-permute-start.2 = (f32[2,18,128]{2,1,0:T(8,128)S(1)}, f32[2,18,128]{2,1,0:T(8,128)S(1)}, u32[]{:S(2)}, u32[]{:S(2)}) collective-permute-start(f32[2,18,128]{2,1,0:T(8,128)S(1)} %get-tuple-element.38), channel_id=1, source_target_pairs={{0,8},{8,0},{1,9},{9,1},{2,10},{10,2},{3,11},{11,3},{4,12},{12,4},... | collective-permute-start | bytes 55304 | tf_op jit(solution)/shard_map/ppermute | solution.py:34
  104.8 10.6 %collective-permute-start.3 = (bf16[112,1152]{1,0:T(8,128)(2,1)S(1)}, bf16[112,1152]{1,0:T(8,128)(2,1)S(1)}, u32[]{:S(2)}, u32[]{:S(2)}) collective-permute-start(bf16[112,1152]{1,0:T(8,128)(2,1)S(1)} %convolution_convert_fusion), channel_id=1, source_target_pairs={{0,8},{8,0},{1,9},{9,1},{2,10},{10,2},{3,11},{11,3},{4,12},{12,4},... | collective-permute-start | bytes 774152 | tf_op jit(solution)/shard_map/ppermute | solution.py:34
